TPU v7x, 1024 devices: a whole 4x4x32 slice. The times are simulated.
1024 devices in a mesh: expert: 16 (over y, x_hi, core), replica: 64 (over x_lo, z).
Axes of the slice: x: 4 (x_hi: 2, x_lo: 2; x = x_hi * 2 + x_lo), y: 4, z: 32, core: 2. Of those that a mesh axis runs over, the one named last changes fastest.
Arguments:
- tokens: bfloat16 [2048, 4096], P('replica', 'expert'), may hold values from -6 to 6
- cotangent: bfloat16 [2048, 4096], P('replica', 'expert'), may hold values from -6 to 6
- route_probs: float32 [2048, 8], P('replica'), may hold values from 0.05 to 0.3
- expert_ids: int32 [2048, 8], P('replica'), may hold values from 0 to 63, all different within a row; in each aligned block of 32 rows (0 to 31, 32 to 63, ...) at most 8 rows name the same one
- seq_ids: int32 [2048], P('replica'), may hold values from 0 to 255, never falling along the last dimension, each value on 1 to 16 neighbouring positions
- ratios: float32 [256], replicated, may hold values from 0.5 to 2
- gate_weight: bfloat16 [64, 4096, 1024], P('replica', 'expert'), may hold values from -0.09375 to 0.09375
- up_weight: bfloat16 [64, 4096, 1024], P('replica', 'expert'), may hold values from -0.09375 to 0.09375
- down_weight: bfloat16 [64, 1024, 4096], P('replica', None, 'expert'), may hold values from -0.1875 to 0.1875
Outputs:
- layer_out: bfloat16 [2048, 4096], P('replica', 'expert')
- grad_tokens: bfloat16 [2048, 4096], P('replica', 'expert')
- grad_gate: bfloat16 [64, 4096, 1024], P('replica', 'expert')
- grad_up: bfloat16 [64, 4096, 1024], P('replica', 'expert')
- grad_down: bfloat16 [64, 1024, 4096], P('replica', None, 'expert')
Inputs may be any that keep to these rules, and one draw needn't show every extreme that they name: `expert_ids`: each token names 8 different experts. Within the 32 tokens of one device (aligned blocks of the token order), no expert is named by more than 8 tokens, a bound that some block reaches. `seq_ids`: never falls along the token order; a sequence holds at most 16 tokens, and some sequence exactly 16.
All inputs are finite; a program needn't handle non-finite values.
Results may differ from a plain program's by a relative error of at most 0.035.
Values may be sent and summed in bfloat16 or wider, within the bound.
No kernel may reach another device: no remote copies, remote signals or barrier semaphores. Data moves between devices by JAX's collectives and lax.ppermute only.
A program may use at most 32 MiB of HBM per device.

v0:
```python
import jax
import jax.numpy as jnp
from jax import lax
from jax.sharding import PartitionSpec as P

clip_low = 0.8
clip_high = 1.25


def silu_parts(gate_sum):
    sigmoid = jax.nn.sigmoid(gate_sum)
    return (gate_sum * sigmoid, sigmoid * (1.0 + gate_sum * (1.0 - sigmoid)))


def routing_table(expert_ids, capacity, expert_count):
    labels = jnp.arange(expert_count, dtype=jnp.int32)
    matches = expert_ids[:, :, None] == labels[None, None, :]
    member = jnp.sum(matches.astype(jnp.int32), axis=1)
    before = jnp.cumsum(member, axis=0) - member
    slot_index = jnp.sum(jnp.where(matches, before[:, None, :], 0), axis=2)
    column = (expert_ids * capacity + slot_index).reshape(-1)
    places = jnp.arange(expert_count * capacity, dtype=jnp.int32)
    return (column[:, None] == places[None, :]).astype(jnp.bfloat16)


def local(
    tokens, cotangent, route_probs, expert_ids, seq_ids, ratios, gate_weight, up_weight, down_weight
):
    token_count = tokens.shape[0]
    feature_width = tokens.shape[1]
    route_count = expert_ids.shape[1]
    local_experts = gate_weight.shape[0]
    sources = lax.axis_size("replica")
    expert_count = local_experts * sources
    capacity = token_count // 4
    routes_table = routing_table(expert_ids, capacity, expert_count)
    sequence_labels = jnp.arange(ratios.shape[0], dtype=jnp.int32)
    picked = jnp.sum(
        jnp.where(seq_ids[:, None] == sequence_labels[None, :], ratios[None, :], 0.0), axis=1
    )
    weights = jnp.clip(picked, clip_low, clip_high)
    scaled = (
        (route_probs * weights[:, None])[:, :, None] * cotangent.astype(jnp.float32)[:, None, :]
    ).astype(jnp.bfloat16)
    repeated = jnp.broadcast_to(tokens[:, None, :], (token_count, route_count, feature_width))
    send_inputs = jnp.einsum(
        "qc,qd->cd",
        routes_table,
        repeated.reshape(-1, feature_width),
        preferred_element_type=jnp.float32,
    ).astype(jnp.bfloat16)
    send_seeds = jnp.einsum(
        "qc,qd->cd",
        routes_table,
        scaled.reshape(-1, feature_width),
        preferred_element_type=jnp.float32,
    ).astype(jnp.bfloat16)
    inputs, seed_rows = (
        lax.all_to_all(
            send_inputs.reshape(expert_count, capacity, feature_width),
            "replica",
            split_axis=0,
            concat_axis=1,
            tiled=True,
        ),
        lax.all_to_all(
            send_seeds.reshape(expert_count, capacity, feature_width),
            "replica",
            split_axis=0,
            concat_axis=1,
            tiled=True,
        ),
    )
    gate_part = jnp.einsum("erd,edh->erh", inputs, gate_weight, preferred_element_type=jnp.float32)
    up_part = jnp.einsum("erd,edh->erh", inputs, up_weight, preferred_element_type=jnp.float32)
    gate_sum, up_sum = (
        lax.psum(gate_part.astype(jnp.bfloat16), "expert").astype(jnp.float32),
        lax.psum(up_part.astype(jnp.bfloat16), "expert").astype(jnp.float32),
    )
    active, slopes = silu_parts(gate_sum)
    hidden = (active * up_sum).astype(jnp.bfloat16)
    outputs = jnp.einsum(
        "erh,ehd->erd", hidden, down_weight, preferred_element_type=jnp.float32
    ).astype(jnp.bfloat16)
    hidden_part = jnp.einsum(
        "erd,ehd->erh", seed_rows, down_weight, preferred_element_type=jnp.float32
    )
    hidden_cot = lax.psum(hidden_part.astype(jnp.bfloat16), "expert").astype(jnp.float32)
    gate_cot = (hidden_cot * up_sum * slopes).astype(jnp.bfloat16)
    up_cot = (hidden_cot * active).astype(jnp.bfloat16)
    back_rows = (
        jnp.einsum("erh,edh->erd", gate_cot, gate_weight, preferred_element_type=jnp.float32)
        + jnp.einsum("erh,edh->erd", up_cot, up_weight, preferred_element_type=jnp.float32)
    ).astype(jnp.bfloat16)
    grad_gate = jnp.einsum(
        "erd,erh->edh", inputs, gate_cot, preferred_element_type=jnp.float32
    ).astype(jnp.bfloat16)
    grad_up = jnp.einsum("erd,erh->edh", inputs, up_cot, preferred_element_type=jnp.float32).astype(
        jnp.bfloat16
    )
    grad_down = jnp.einsum(
        "erh,erd->ehd", hidden, seed_rows, preferred_element_type=jnp.float32
    ).astype(jnp.bfloat16)
    came_out, came_back = (
        lax.all_to_all(outputs, "replica", split_axis=1, concat_axis=0, tiled=True),
        lax.all_to_all(back_rows, "replica", split_axis=1, concat_axis=0, tiled=True),
    )
    out_routes = jnp.einsum(
        "qc,cd->qd",
        routes_table,
        came_out.reshape(expert_count * capacity, feature_width),
        preferred_element_type=jnp.float32,
    ).reshape(token_count, route_count, feature_width)
    layer_out = jnp.sum(route_probs[:, :, None] * out_routes, axis=1).astype(jnp.bfloat16)
    back_routes = jnp.einsum(
        "qc,cd->qd",
        routes_table,
        came_back.reshape(expert_count * capacity, feature_width),
        preferred_element_type=jnp.float32,
    ).reshape(token_count, route_count, feature_width)
    grad_tokens = jnp.sum(back_routes, axis=1).astype(jnp.bfloat16)
    return (layer_out, grad_tokens, grad_gate, grad_up, grad_down)


def solution(mesh):
    return jax.shard_map(
        local,
        mesh=mesh,
        in_specs=(
            P("replica", "expert"),
            P("replica", "expert"),
            P("replica", None),
            P("replica", None),
            P("replica"),
            P(),
            P("replica", "expert", None),
            P("replica", "expert", None),
            P("replica", None, "expert"),
        ),
        out_specs=(
            P("replica", "expert"),
            P("replica", "expert"),
            P("replica", "expert", None),
            P("replica", "expert", None),
            P("replica", None, "expert"),
        ),
        check_vma=False,
    )
```

profile of v0, /device:TPU:1, one launch (start us, length us, event | category | flops | bytes accessed | tf_op | source)
XLA Modules:
  0.0 423.2 jit_solution(11252088624260096733)
XLA Ops:
  9.0 1.8 fusion.16
  10.9 30.8 %all-to-all-start = ((bf16[64,8,256]{2,1,0:T(8,128)(2,1)}), bf16[64,8,256]{2,1,0:T(8,128)(2,1)S(1)}, u32[]{:S(2)}, u32[]{:S(2)}) async-start(bf16[64,8,256]{2,1,0:T(8,128)(2,1)} %fusion.16), calls=%async_computation | async-start | bytes 524288 | tf_op jit(solution)/shard_map/all_to_all | solution.py:59
  42.1 1.1 fusion.17
  43.3 35.6 %all-to-all-done = bf16[64,8,256]{2,1,0:T(8,128)(2,1)S(1)} async-done(((bf16[64,8,256]{2,1,0:T(8,128)(2,1)}), bf16[64,8,256]{2,1,0:T(8,128)(2,1)S(1)}, u32[]{:S(2)}, u32[]{:S(2)}) %all-to-all-start) | async-done | bytes 262176 | tf_op jit(solution)/shard_map/all_to_all | solution.py:59
  78.8 8.8 %all-to-all-start.2 = ((bf16[64,8,256]{2,1,0:T(8,128)(2,1)}), bf16[64,8,256]{2,1,0:T(8,128)(2,1)S(1)}, u32[]{:S(2)}, u32[]{:S(2)}) async-start(bf16[64,8,256]{2,1,0:T(8,128)(2,1)} %fusion.17), calls=%async_computation.2 | async-start | bytes 524288 | tf_op jit(solution)/shard_map/all_to_all | solution.py:66
  87.7 1.4 fusion.10
  89.1 1.4 fusion.9
  90.6 33.8 %all-to-all-done.2 = bf16[64,8,256]{2,1,0:T(8,128)(2,1)S(1)} async-done(((bf16[64,8,256]{2,1,0:T(8,128)(2,1)}), bf16[64,8,256]{2,1,0:T(8,128)(2,1)S(1)}, u32[]{:S(2)}, u32[]{:S(2)}) %all-to-all-start.2) | async-done | bytes 262176 | tf_op jit(solution)/shard_map/all_to_all | solution.py:66
  124.4 1.5 fusion.11
  125.9 174.1 %all-reduce.3.cloned.1.call-done = (bf16[1,512,1024]{2,1,0:T(8,128)(2,1)}, bf16[1,512,1024]{2,1,0:T(8,128)(2,1)}, bf16[1,512,1024]{2,1,0:T(8,128)(2,1)}) async-done(((bf16[1,512,1024]{2,1,0:T(8,128)(2,1)}, bf16[1,512,1024]{2,1,0:T(8,128)(2,1)}, bf16[1,512,1024]{2,1,0:T(8,128)(2,1)}), (bf16[1,512,1024]{2,1,0:T(8,128)(2,1)}, bf16[1,512,1024]{2,1,0:T(8,128)(2,1)}, ...) | async-done | bytes 3145744 | tf_op jit(solution)/shard_map/psum | solution.py:78
  300.1 4.2 %fusion.21 = (bf16[512,1024]{1,0:T(8,128)(2,1)S(1)}, bf16[1,512,1024]{2,1,0:T(8,128)(2,1)S(1)}, bf16[512,1024]{1,0:T(8,128)(2,1)}) fusion(bf16[1,512,1024]{2,1,0:T(8,128)(2,1)} %get-tuple-element.7, bf16[1,512,1024]{2,1,0:T(8,128)(2,1)} %get-tuple-element.6, bf16[1,512,1024]{2,1,0:T(8,128)(2,1)} %get-tuple-element.5), kind=kLoop, calls=%fused_computation.39 | loop fusion | flops 9437184 | bytes 6291456 | tf_op jit(solution)/shard_map/reshape.36
  306.2 2.9 reduce.1
  309.1 1.8 reshape.175
  310.9 23.0 %all-to-all-start.3 = ((bf16[64,2,1024]{2,1,0:T(2,128)(2,1)}), bf16[64,2,1024]{2,1,0:T(2,128)(2,1)}, u32[]{:S(2)}, u32[]{:S(2)}) async-start(bf16[64,2,1024]{2,1,0:T(2,128)(2,1)} %reshape.175), calls=%async_computation.3 | async-start | bytes 524288 | tf_op jit(solution)/shard_map/all_to_all | solution.py:106
  333.9 1.7 fusion.18
  336.0 2.9 reduce
  338.9 1.7 reshape.173
  340.7 28.7 %all-to-all-done.3 = bf16[64,2,1024]{2,1,0:T(2,128)(2,1)} async-done(((bf16[64,2,1024]{2,1,0:T(2,128)(2,1)}), bf16[64,2,1024]{2,1,0:T(2,128)(2,1)}, u32[]{:S(2)}, u32[]{:S(2)}) %all-to-all-start.3) | async-done | bytes 262176 | tf_op jit(solution)/shard_map/all_to_all | solution.py:106
  369.3 9.7 %all-to-all-start.1 = ((bf16[64,2,1024]{2,1,0:T(2,128)(2,1)}), bf16[64,2,1024]{2,1,0:T(2,128)(2,1)S(1)}, u32[]{:S(2)}, u32[]{:S(2)}) async-start(bf16[64,2,1024]{2,1,0:T(2,128)(2,1)} %reshape.173), calls=%async_computation.1 | async-start | bytes 524288 | tf_op jit(solution)/shard_map/all_to_all | solution.py:105
  379.2 1.3 fusion.12
  380.4 1.3 fusion.13
  381.7 1.3 fusion.14
  383.0 2.1 reshape.176
  386.1 29.1 %all-to-all-done.1 = bf16[64,2,1024]{2,1,0:T(2,128)(2,1)S(1)} async-done(((bf16[64,2,1024]{2,1,0:T(2,128)(2,1)}), bf16[64,2,1024]{2,1,0:T(2,128)(2,1)S(1)}, u32[]{:S(2)}, u32[]{:S(2)}) %all-to-all-start.1) | async-done | bytes 262176 | tf_op jit(solution)/shard_map/all_to_all | solution.py:105
  (46 shorter events, 6.7 us)
Async XLA Ops:
  7.2 82.0 %copy-start = (bf16[1,256,1024]{2,1,0:T(8,128)(2,1)S(1)}, bf16[1,256,1024]{2,1,0:T(8,128)(2,1)}, u32[]{:S(2)}) copy-start(bf16[1,256,1024]{2,1,0:T(8,128)(2,1)} %param.15) | copy-start | bytes 1572868
  7.2 34.5 %copy-start.7 = (bf16[32,256]{1,0:T(8,128)(2,1)S(1)}, bf16[32,256]{1,0:T(8,128)(2,1)}, u32[]{:S(2)}) copy-start(bf16[32,256]{1,0:T(8,128)(2,1)} %param.10) | copy-start | bytes 49156
  7.2 34.6 %copy-start.10 = (s32[32]{0:T(128)S(1)}, s32[32]{0:T(128)}, u32[]{:S(2)}) copy-start(s32[32]{0:T(128)} %param.13) | copy-start | bytes 388
  7.2 34.6 %copy-start.9 = (f32[256]{0:T(256)S(1)}, f32[256]{0:T(256)}, u32[]{:S(2)}) copy-start(f32[256]{0:T(256)} %param.14) | copy-start | bytes 3076
  7.2 34.7 %copy-start.8 = (f32[32,8]{0,1:T(8,128)S(1)}, f32[32,8]{0,1:T(8,128)}, u32[]{:S(2)}) copy-start(f32[32,8]{0,1:T(8,128)} %param.11) | copy-start | bytes 3076
  7.2 80.5 %copy-start.1 = (bf16[1,256,1024]{2,1,0:T(8,128)(2,1)S(1)}, bf16[1,256,1024]{2,1,0:T(8,128)(2,1)}, u32[]{:S(2)}) copy-start(bf16[1,256,1024]{2,1,0:T(8,128)(2,1)} %param.16) | copy-start | bytes 1572868
  10.9 68.0 %all-to-all-start = ((bf16[64,8,256]{2,1,0:T(8,128)(2,1)}), bf16[64,8,256]{2,1,0:T(8,128)(2,1)S(1)}, u32[]{:S(2)}, u32[]{:S(2)}) async-start(bf16[64,8,256]{2,1,0:T(8,128)(2,1)} %fusion.16), calls=%async_computation | async-start | bytes 524288 | tf_op jit(solution)/shard_map/all_to_all | solution.py:59
  78.8 45.6 %all-to-all-start.2 = ((bf16[64,8,256]{2,1,0:T(8,128)(2,1)}), bf16[64,8,256]{2,1,0:T(8,128)(2,1)S(1)}, u32[]{:S(2)}, u32[]{:S(2)}) async-start(bf16[64,8,256]{2,1,0:T(8,128)(2,1)} %fusion.17), calls=%async_computation.2 | async-start | bytes 524288 | tf_op jit(solution)/shard_map/all_to_all | solution.py:66
  87.7 212.4 %all-reduce.3.cloned.1.call-start = ((), (), s32[]{:S(2)}) async-start(), calls=%async_computation.4 | async-start | bytes 6291456 | tf_op jit(solution)/shard_map/psum | solution.py:78
  89.1 35.3 %copy-start.5 = (bf16[1,1024,256]{2,1,0:T(8,128)(2,1)S(1)}, bf16[1,1024,256]{2,1,0:T(8,128)(2,1)}, u32[]{:S(2)}) copy-start(bf16[1,1024,256]{2,1,0:T(8,128)(2,1)} %param.17) | copy-start | bytes 1572868
  124.4 1.5 copy-start.2
  309.1 24.8 %copy-start.6 = (bf16[1,1024,256]{2,1,0:T(8,128)(2,1)S(1)}, bf16[1,1024,256]{2,1,0:T(8,128)(2,1)}, u32[]{:S(2)}) copy-start(bf16[1,1024,256]{2,1,0:T(8,128)(2,1)} %param.17) | copy-start | bytes 1572868
  310.9 58.4 %all-to-all-start.3 = ((bf16[64,2,1024]{2,1,0:T(2,128)(2,1)}), bf16[64,2,1024]{2,1,0:T(2,128)(2,1)}, u32[]{:S(2)}, u32[]{:S(2)}) async-start(bf16[64,2,1024]{2,1,0:T(2,128)(2,1)} %reshape.175), calls=%async_computation.3 | async-start | bytes 524288 | tf_op jit(solution)/shard_map/all_to_all | solution.py:106
  369.3 45.9 %all-to-all-start.1 = ((bf16[64,2,1024]{2,1,0:T(2,128)(2,1)}), bf16[64,2,1024]{2,1,0:T(2,128)(2,1)S(1)}, u32[]{:S(2)}, u32[]{:S(2)}) async-start(bf16[64,2,1024]{2,1,0:T(2,128)(2,1)} %reshape.173), calls=%async_computation.1 | async-start | bytes 524288 | tf_op jit(solution)/shard_map/all_to_all | solution.py:105
  380.4 1.3 copy-start.3
  380.4 1.3 copy-start.4
Sparse Core Ops, SparseCore 0:
  126.0 173.9 all-reduce.2
where the time goes:
time: 427 us; the launch traced here: 423 us
  waiting for transfers between devices  301 us (70%)
  starting transfers between devices  72.4 us (17%)
  matrix products  15.6 us (4%)
  between operations  14.3 us (3%)
  other arithmetic  11.1 us (3%)
  local copies, waits for them, and re-layouts  8.49 us (2%)
    psum x1, waiting for transfers between devices, local(): lax.psum(up_part.astype(jnp.bfloat16), 'expert').astype(jnp.float32)  174 us
    all_to_all x1, waiting for transfers between devices, local(): lax.all_to_all(send_inputs.reshape(expert_count, capacity, feature_width)...  35.6 us
    all_to_all x1, waiting for transfers between devices, local(): lax.all_to_all(send_seeds.reshape(expert_count, capacity, feature_width),...  33.8 us
    all_to_all x1, starting transfers between devices, local(): lax.all_to_all(send_inputs.reshape(expert_count, capacity, feature_width)...  30.8 us
    all_to_all x1, waiting for transfers between devices, local(): lax.all_to_all(outputs, 'replica', split_axis=1, concat_axis=0, tiled=True)  29.1 us
    all_to_all x1, waiting for transfers between devices, local(): lax.all_to_all(back_rows, 'replica', split_axis=1, concat_axis=0, tiled=T...  28.7 us
    all_to_all x1, starting transfers between devices, local(): lax.all_to_all(back_rows, 'replica', split_axis=1, concat_axis=0, tiled=T...  23 us
    all_to_all x1, starting transfers between devices, local(): lax.all_to_all(outputs, 'replica', split_axis=1, concat_axis=0, tiled=True)  9.74 us
  transfers between devices with their start and end apart: 5, of which 5 were waited for; matrix products, arithmetic and copies ran while one was open for 4% of the time, Pallas kernels for 0%

commit v1 on v0

v1 whole, which is shorter than its diff:
```python
import jax
import jax.numpy as jnp
from jax import lax
from jax.experimental import pallas as pl
from jax.experimental.pallas import tpu as pltpu
from jax.sharding import PartitionSpec as P

clip_low = 0.8
clip_high = 1.25

bf16 = jnp.bfloat16
f32 = jnp.float32

NN = (((1,), (0,)), ((), ()))
NT = (((1,), (1,)), ((), ()))
TN = (((0,), (0,)), ((), ()))


def mm(a, b, dims):
    return lax.dot_general(a, b, dims, preferred_element_type=f32)


def call(body, outs, flops, nbytes, **more):
    return pl.pallas_call(
        body,
        out_shape=outs,
        cost_estimate=pl.CostEstimate(flops=flops, bytes_accessed=nbytes, transcendentals=0),
        compiler_params=pltpu.CompilerParams(vmem_limit_bytes=40 * 1024 * 1024),
        **more,
    )


def pieces(x):
    first = x.astype(bf16)
    rest = x - first.astype(f32)
    second = rest.astype(bf16)
    third = (rest - second.astype(f32)).astype(bf16)
    return jnp.concatenate([first, second, third], axis=0)


def pack_kernel(tokens_ref, cot_ref, probs_ref, ids_ref, seq_ref, ratios_ref, send_ref, table_ref):
    count, width = tokens_ref.shape
    routes = ids_ref.shape[1]
    places = send_ref.shape[0]
    capacity = 8
    rows = lax.broadcasted_iota(jnp.int32, (count, count), 0)
    cols = lax.broadcasted_iota(jnp.int32, (count, count), 1)
    seq_row = seq_ref[...].astype(f32)
    seq_col = jnp.sum(jnp.where(rows == cols, seq_row, 0.0), axis=1, keepdims=True)
    labels = lax.broadcasted_iota(jnp.int32, (count, ratios_ref.shape[1]), 1).astype(f32)
    picked = jnp.sum(jnp.where(labels == seq_col, ratios_ref[...], 0.0), axis=1, keepdims=True)
    weights = jnp.clip(picked, clip_low, clip_high)
    probs = probs_ref[...]
    scaled = probs * weights
    ids = ids_ref[...]
    place = lax.broadcasted_iota(jnp.int32, (count, places), 1)
    owner = place // capacity
    member = jnp.zeros((count, places), f32)
    prob_at = jnp.zeros((count, places), f32)
    scale_at = jnp.zeros((count, places), f32)
    for k in range(routes):
        named = ids[:, k : k + 1] == owner
        member = jnp.where(named, 1.0, member)
        prob_at = jnp.where(named, probs[:, k : k + 1], prob_at)
        scale_at = jnp.where(named, scaled[:, k : k + 1], scale_at)
    lower = jnp.where(rows > cols, 1.0, 0.0).astype(bf16)
    before = mm(lower, member.astype(bf16), NN)
    here = (member > 0.0) & (before == (place % capacity).astype(f32))
    table = jnp.where(here, 1.0, 0.0).astype(bf16)
    table_ref[0 : 3 * count, :] = pieces(jnp.where(here, prob_at, 0.0))
    table_ref[3 * count : 4 * count, :] = table
    cot = cot_ref[...]
    send_ref[:, 0:width] = mm(table, tokens_ref[...], TN).astype(bf16)
    seeds = mm(
        pieces(jnp.where(here, scale_at, 0.0)), jnp.concatenate([cot, cot, cot], axis=0), TN
    )
    send_ref[:, width : 2 * width] = seeds.astype(bf16)


def partial_kernel(flip, rows_ref, gate_ref, up_ref, down_ref, out_ref):
    half = out_ref.shape[0]
    width = gate_ref.shape[0]
    hidden = gate_ref.shape[1]
    side = (lax.axis_index("expert") + flip) % 2
    at = pl.ds(pl.multiple_of(side * half, half), half)
    inputs = rows_ref[at, 0:width]
    seeds = rows_ref[at, width : 2 * width]
    out_ref[:, 0:hidden] = mm(inputs, gate_ref[...], NN).astype(bf16)
    out_ref[:, hidden : 2 * hidden] = mm(inputs, up_ref[...], NN).astype(bf16)
    out_ref[:, 2 * hidden : 3 * hidden] = mm(seeds, down_ref[...], NT).astype(bf16)


def add_kernel(a_ref, b_ref, out_ref):
    out_ref[...] = (a_ref[...].astype(f32) + b_ref[...].astype(f32)).astype(bf16)


def middle_kernel(parts_ref, out_ref):
    groups, rows, wide = parts_ref.shape
    hidden = wide // 3
    total = parts_ref[0].astype(f32)
    for g in range(1, groups):
        total = total + parts_ref[g].astype(f32)
    gate_sum = total[:, 0:hidden]
    up_sum = total[:, hidden : 2 * hidden]
    hidden_cot = total[:, 2 * hidden : 3 * hidden]
    sigmoid = 1.0 / (1.0 + jnp.exp(-gate_sum))
    active = gate_sum * sigmoid
    slopes = sigmoid * (1.0 + gate_sum * (1.0 - sigmoid))
    inner = (active * up_sum).astype(bf16)
    gate_cot = (hidden_cot * up_sum * slopes).astype(bf16)
    up_cot = (hidden_cot * active).astype(bf16)
    for g in range(groups):
        out_ref[g, :, 0:hidden] = inner
        out_ref[g, :, hidden : 2 * hidden] = gate_cot
        out_ref[g, :, 2 * hidden : 3 * hidden] = up_cot


def back_half(hgu_ref, gate_ref, up_ref, down_ref):
    hidden = gate_ref.shape[1]
    out = mm(hgu_ref[:, 0:hidden], down_ref[...], NN).astype(bf16)
    back = mm(hgu_ref[:, hidden : 2 * hidden], gate_ref[...], NT) + mm(
        hgu_ref[:, 2 * hidden : 3 * hidden], up_ref[...], NT
    )
    return out, back.astype(bf16)


def own_back_kernel(hgu_ref, gate_ref, up_ref, down_ref, out_ref):
    width = gate_ref.shape[0]
    out, back = back_half(hgu_ref, gate_ref, up_ref, down_ref)
    out_ref[:, 0:width] = out
    out_ref[:, width : 2 * width] = back


def other_back_kernel(own_ref, hgu_ref, gate_ref, up_ref, down_ref, out_ref):
    width = gate_ref.shape[0]
    half = own_ref.shape[0]
    core = lax.axis_index("expert") % 2
    mine = pl.ds(pl.multiple_of(core * half, half), half)
    theirs = pl.ds(pl.multiple_of((1 - core) * half, half), half)
    out_ref[mine, :] = own_ref[...]
    out, back = back_half(hgu_ref, gate_ref, up_ref, down_ref)
    out_ref[theirs, 0:width] = out
    out_ref[theirs, width : 2 * width] = back


def grads_kernel(rows_ref, own_ref, other_ref, grad_gate_ref, grad_up_ref, grad_down_ref):
    width, hidden = grad_gate_ref.shape
    half = own_ref.shape[0]
    core = lax.axis_index("expert") % 2
    mine = pl.ds(pl.multiple_of(core * half, half), half)
    theirs = pl.ds(pl.multiple_of((1 - core) * half, half), half)

    def both(columns, hgu):
        return mm(rows_ref[mine, columns], own_ref[:, hgu], TN) + mm(
            rows_ref[theirs, columns], other_ref[:, hgu], TN
        )

    inputs = slice(0, width)
    seeds = slice(width, 2 * width)
    grad_gate_ref[...] = both(inputs, slice(hidden, 2 * hidden)).astype(bf16)
    grad_up_ref[...] = both(inputs, slice(2 * hidden, 3 * hidden)).astype(bf16)
    inner = slice(0, hidden)
    grad_down_ref[...] = (
        mm(own_ref[:, inner], rows_ref[mine, seeds], TN)
        + mm(other_ref[:, inner], rows_ref[theirs, seeds], TN)
    ).astype(bf16)


def combine_kernel(table_ref, came_ref, out_ref, grad_ref):
    count, width = out_ref.shape
    parts = mm(table_ref[0 : 3 * count, :], came_ref[:, 0:width], NN)
    out_ref[...] = (
        parts[0:count] + parts[count : 2 * count] + parts[2 * count : 3 * count]
    ).astype(bf16)
    grad_ref[...] = mm(
        table_ref[3 * count : 4 * count, :], came_ref[:, width : 2 * width], NN
    ).astype(bf16)


def local(
    tokens, cotangent, route_probs, expert_ids, seq_ids, ratios, gate_weight, up_weight, down_weight
):
    count, width = tokens.shape
    hidden = gate_weight.shape[2]
    sources = lax.axis_size("replica")
    groups = lax.axis_size("expert")
    capacity = count // 4
    places = sources * capacity
    half = places // 2
    gate, up, down = gate_weight[0], up_weight[0], down_weight[0]
    shape = jax.ShapeDtypeStruct
    swap = [(i, i ^ 1) for i in range(groups)]
    sides = [list(range(0, groups, 2)), list(range(1, groups, 2))]
    product = 2 * half * width * hidden

    def spread(x, axis, index_groups=None):
        return lax.all_to_all(
            x, axis, split_axis=0, concat_axis=0, axis_index_groups=index_groups, tiled=True
        )

    send, table = call(
        pack_kernel,
        (shape((places, 2 * width), bf16), shape((4 * count, places), bf16)),
        2 * places * 4 * count * width,
        2 * places * 2 * width,
    )(
        tokens,
        cotangent,
        route_probs,
        expert_ids,
        seq_ids.reshape(1, count),
        ratios.reshape(1, -1),
    )
    rows = spread(send.reshape(sources, capacity, 2 * width), "replica").reshape(places, 2 * width)

    def partial(flip):
        return call(
            lambda *refs: partial_kernel(flip, *refs),
            shape((half, 3 * hidden), bf16),
            3 * product,
            2 * (half * 3 * hidden + 3 * width * hidden),
        )(rows, gate, up, down)

    came = lax.ppermute(partial(1), "expert", swap)
    mine = partial(0)
    summed = call(
        add_kernel, shape((half, 3 * hidden), bf16), half * 3 * hidden, 6 * half * 3 * hidden
    )(mine, came)
    eighth = half // (groups // 2)
    parts = spread(summed.reshape(groups // 2, eighth, 3 * hidden), "expert", sides)
    copies = call(
        middle_kernel,
        shape((groups // 2, eighth, 3 * hidden), bf16),
        20 * half * 3 * hidden,
        4 * half * 3 * hidden,
    )(parts)
    own = spread(copies, "expert", sides).reshape(half, 3 * hidden)
    other = lax.ppermute(own, "expert", swap)
    own_back = call(
        own_back_kernel, shape((half, 2 * width), bf16), 3 * product, 2 * 3 * width * hidden
    )(own, gate, up, down)
    back = call(
        other_back_kernel, shape((places, 2 * width), bf16), 3 * product, 2 * 3 * width * hidden
    )(own_back, other, gate, up, down)
    returned = spread(back.reshape(sources, capacity, 2 * width), "replica")
    grads = call(
        grads_kernel,
        (
            shape((width, hidden), bf16),
            shape((width, hidden), bf16),
            shape((hidden, width), bf16),
        ),
        6 * product,
        2 * 12 * width * hidden,
    )(rows, own, other)
    layer_out, grad_tokens = call(
        combine_kernel,
        (shape((count, width), bf16), shape((count, width), bf16)),
        2 * places * 4 * count * width,
        2 * places * 2 * width,
    )(table, returned.reshape(places, 2 * width))
    return (layer_out, grad_tokens) + tuple(g[None] for g in grads)


def solution(mesh):
    return jax.shard_map(
        local,
        mesh=mesh,
        in_specs=(
            P("replica", "expert"),
            P("replica", "expert"),
            P("replica", None),
            P("replica", None),
            P("replica"),
            P(),
            P("replica", "expert", None),
            P("replica", "expert", None),
            P("replica", None, "expert"),
        ),
        out_specs=(
            P("replica", "expert"),
            P("replica", "expert"),
            P("replica", "expert", None),
            P("replica", "expert", None),
            P("replica", None, "expert"),
        ),
        check_vma=False,
    )
```

time: 427 us -> 236 us (0.55)
  waiting for transfers between devices: 301 us -> 57.9 us
  blocking collectives: 0 us -> 139 us
  starting transfers between devices: 72.4 us -> 19.7 us
  matrix products: 15.6 us -> 0 us
  between operations: 14.3 us -> 0.75 us
  other arithmetic: 11.1 us -> 0 us
  Pallas kernels: 0 us -> 6.29 us
    psum x1 -> x0, waiting for transfers between devices: 174 us -> none  [local(): lax.psum(up_part.astype(jnp.bfloat16), 'expert').astype(jnp.float32)]
    all_to_all x0 -> x3, blocking collectives: none -> 139 us  [spread(): lax.all_to_all(x, axis, split_axis=0, concat_axis=0, axis_index_groups=in...]
    all_to_all x4 -> x1, waiting for transfers between devices: 127 us -> 53 us  [spread(): lax.all_to_all(x, axis, split_axis=0, concat_axis=0, axis_index_groups=in...]
    all_to_all x4 -> x1, starting transfers between devices: 72.3 us -> 10.4 us  [spread(): lax.all_to_all(x, axis, split_axis=0, concat_axis=0, axis_index_groups=in...]
    dot_general x13 -> x0, matrix products: 15.6 us -> none  [the longest x1 1.84 us: local(): jnp.einsum('qc,qd->cd', routes_table, repeated.reshape(-1, feature_width)...]
    ppermute x0 -> x2, starting transfers between devices: none -> 9.25 us  [the longest x1 4.98 us: local(): came = lax.ppermute(partial(1), 'expert', swap)]
    pallas_call x0 -> x9, Pallas kernels: none -> 6.29 us  [the longest x1 1.82 us: local(): call(grads_kernel, (shape((width, hidden), bf16), shape((width, hidden),...]
    unnamed x2 -> x0, other arithmetic: 5.83 us -> none
  transfers between devices with their start and end apart: 5 -> 3, of which waited for: 5 -> 3; matrix products, arithmetic and copies ran while one was open for 4% -> 0% of each run, Pallas kernels for 0% -> 1%
where the time goes in v1:
time: 236 us; the launch traced here: 232 us
  blocking collectives  139 us (59%)
  waiting for transfers between devices  57.9 us (25%)
  starting transfers between devices  19.7 us (8%)
  local copies, waits for them, and re-layouts  8.24 us (3%)
  Pallas kernels  6.29 us (3%)
    all_to_all x3, blocking collectives, spread(): lax.all_to_all(x, axis, split_axis=0, concat_axis=0, axis_index_groups=in...  139 us
    all_to_all x1, waiting for transfers between devices, spread(): lax.all_to_all(x, axis, split_axis=0, concat_axis=0, axis_index_groups=in...  53 us
    all_to_all x1, starting transfers between devices, spread(): lax.all_to_all(x, axis, split_axis=0, concat_axis=0, axis_index_groups=in...  10.4 us
    unnamed x24, local copies, waits for them, and re-layouts  8.24 us
    ppermute x1, starting transfers between devices, local(): came = lax.ppermute(partial(1), 'expert', swap)  4.98 us
  transfers between devices with their start and end apart: 3, of which 3 were waited for; matrix products, arithmetic and copies ran while one was open for 0% of the time, Pallas kernels for 1%

profile of v1, /device:TPU:1, one launch (start us, length us, event | category | flops | bytes accessed | tf_op | source)
XLA Modules:
  0.0 231.9 jit_solution(5887050463419789566)
XLA Ops:
  0.7 0.8 copy.14.probs_ref
  1.5 0.8 copy.15.ids_ref
  2.3 0.7 copy-done.7
  3.0 0.7 copy-done.8
  3.7 0.7 copy-done.9
  4.4 0.7 copy-done.10
  5.0 0.7 shard_map.128
  5.7 86.6 %all_to_all.20 = bf16[64,8,512]{2,1,0:T(8,128)(2,1)S(1)} all-to-all(bf16[64,8,512]{2,1,0:T(8,128)(2,1)S(1)} %bitcast.35), channel_id=1, replica_groups=mesh['expert'=16,'replica'=64] {'replica'}, dimensions={0} | all-to-all | bytes 1048576 | tf_op jit(solution)/shard_map/all_to_all | solution.py:197
  92.3 1.0 copy-done.2
  93.9 5.0 %collective-permute-start = (bf16[256,3072]{1,0:T(8,128)(2,1)S(1)}, bf16[256,3072]{1,0:T(8,128)(2,1)S(1)}, u32[]{:S(2)}, u32[]{:S(2)}) collective-permute-start(bf16[256,3072]{1,0:T(8,128)(2,1)S(1)} %shard_map.130), channel_id=1, source_target_pairs={{0,64},{64,0},{128,192},{192,128},{256,320},{320,256},{384,448},{4... | collective-permute-start | bytes 4718600 | tf_op jit(solution)/shard_map/ppermute | solution.py:224
  99.5 2.4 %collective-permute-done.b_ref = bf16[256,3072]{1,0:T(8,128)(2,1)S(1)} collective-permute-done((bf16[256,3072]{1,0:T(8,128)(2,1)S(1)}, bf16[256,3072]{1,0:T(8,128)(2,1)S(1)}, u32[]{:S(2)}, u32[]{:S(2)}) %collective-permute-start) | collective-permute-done | bytes 1572896 | tf_op jit(solution)/shard_map/ppermute | solution.py:224
  102.3 28.1 %all_to_all.21.parts_ref = bf16[8,32,3072]{2,1,0:T(8,128)(2,1)S(1)} all-to-all(bf16[8,32,3072]{2,1,0:T(8,128)(2,1)S(1)} %bitcast.32), channel_id=1, replica_groups={{0,128,256,384,512,640,768,896},{64,192,320,448,576,704,832,960},{1,129..., dimensions={0} | all-to-all | bytes 3145728 | tf_op jit(solution)/shard_map/all_to_all | solution.py:197
  130.7 24.4 %all_to_all.22 = bf16[8,32,3072]{2,1,0:T(8,128)(2,1)S(1)} all-to-all(bf16[8,32,3072]{2,1,0:T(8,128)(2,1)S(1)} %shard_map.132), channel_id=1, replica_groups={{0,128,256,384,512,640,768,896},{64,192,320,448,576,704,832,960},{1,129..., dimensions={0} | all-to-all | bytes 3145728 | tf_op jit(solution)/shard_map/all_to_all | solution.py:197
  155.1 4.3 %collective-permute-start.1 = (bf16[256,3072]{1,0:T(8,128)(2,1)S(1)}, bf16[256,3072]{1,0:T(8,128)(2,1)S(1)}, u32[]{:S(2)}, u32[]{:S(2)}) collective-permute-start(bf16[256,3072]{1,0:T(8,128)(2,1)S(1)} %bitcast.14), channel_id=1, source_target_pairs={{0,64},{64,0},{128,192},{192,128},{256,320},{320,256},{384,448},{4... | collective-permute-start | bytes 4718600 | tf_op jit(solution)/shard_map/ppermute | solution.py:238
  159.4 0.6 shard_map.133.own_ref
  160.0 2.4 %collective-permute-done.1.hgu_ref.other_ref = bf16[256,3072]{1,0:T(8,128)(2,1)S(1)} collective-permute-done((bf16[256,3072]{1,0:T(8,128)(2,1)S(1)}, bf16[256,3072]{1,0:T(8,128)(2,1)S(1)}, u32[]{:S(2)}, u32[]{:S(2)}) %collective-permute-start.1) | collective-permute-done | bytes 1572896 | tf_op jit(solution)/shard_map/ppermute | solution.py:238
  162.4 0.6 shard_map.134
  163.0 0.6 copy-done.4
  163.6 0.8 copy-done.6
  164.4 10.4 %all-to-all-start.3 = ((bf16[64,8,512]{2,1,0:T(8,128)(2,1)}), bf16[64,8,512]{2,1,0:T(8,128)(2,1)S(1)}, u32[]{:S(2)}, u32[]{:S(2)}) async-start(bf16[64,8,512]{2,1,0:T(8,128)(2,1)} %bitcast.33), calls=%async_computation.3 | async-start | bytes 1048576 | tf_op jit(solution)/shard_map/all_to_all | solution.py:197
  174.9 1.4 copy-done.5
  176.3 1.8 shard_map.136
  178.1 53.0 %all-to-all-done.3 = bf16[64,8,512]{2,1,0:T(8,128)(2,1)S(1)} async-done(((bf16[64,8,512]{2,1,0:T(8,128)(2,1)}), bf16[64,8,512]{2,1,0:T(8,128)(2,1)S(1)}, u32[]{:S(2)}, u32[]{:S(2)}) %all-to-all-start.3) | async-done | bytes 524320 | tf_op jit(solution)/shard_map/all_to_all | solution.py:197
  231.1 0.8 shard_map.135
  (18 shorter events, 1.8 us)
Async XLA Ops:
  0.6 91.7 %copy-start = (bf16[1,256,1024]{2,1,0:T(8,128)(2,1)S(1)}, bf16[1,256,1024]{2,1,0:T(8,128)(2,1)}, u32[]{:S(2)}) copy-start(bf16[1,256,1024]{2,1,0:T(8,128)(2,1)} %param.15) | copy-start | bytes 1572868
  0.6 91.7 %copy-start.1 = (bf16[1,256,1024]{2,1,0:T(8,128)(2,1)S(1)}, bf16[1,256,1024]{2,1,0:T(8,128)(2,1)}, u32[]{:S(2)}) copy-start(bf16[1,256,1024]{2,1,0:T(8,128)(2,1)} %param.16) | copy-start | bytes 1572868
  2.3 0.7 copy-start.7
  3.0 0.7 copy-start.8
  3.7 0.7 copy-start.9
  4.4 0.7 copy-start.10
  92.3 1.0 copy-start.2
  93.9 8.0 %collective-permute-start = (bf16[256,3072]{1,0:T(8,128)(2,1)S(1)}, bf16[256,3072]{1,0:T(8,128)(2,1)S(1)}, u32[]{:S(2)}, u32[]{:S(2)}) collective-permute-start(bf16[256,3072]{1,0:T(8,128)(2,1)S(1)} %shard_map.130), channel_id=1, source_target_pairs={{0,64},{64,0},{128,192},{192,128},{256,320},{320,256},{384,448},{4... | collective-permute-start | bytes 4718600 | tf_op jit(solution)/shard_map/ppermute | solution.py:224
  130.7 28.7 %copy-start.3 = (bf16[1,1024,256]{2,1,0:T(8,128)(2,1)S(1)}, bf16[1,1024,256]{2,1,0:T(8,128)(2,1)}, u32[]{:S(2)}) copy-start(bf16[1,1024,256]{2,1,0:T(8,128)(2,1)} %param.17) | copy-start | bytes 1572868
  155.1 7.3 %collective-permute-start.1 = (bf16[256,3072]{1,0:T(8,128)(2,1)S(1)}, bf16[256,3072]{1,0:T(8,128)(2,1)S(1)}, u32[]{:S(2)}, u32[]{:S(2)}) collective-permute-start(bf16[256,3072]{1,0:T(8,128)(2,1)S(1)} %bitcast.14), channel_id=1, source_target_pairs={{0,64},{64,0},{128,192},{192,128},{256,320},{320,256},{384,448},{4... | collective-permute-start | bytes 4718600 | tf_op jit(solution)/shard_map/ppermute | solution.py:238
  162.4 1.2 copy-start.4
  163.6 0.8 copy-start.6
  164.4 66.7 %all-to-all-start.3 = ((bf16[64,8,512]{2,1,0:T(8,128)(2,1)}), bf16[64,8,512]{2,1,0:T(8,128)(2,1)S(1)}, u32[]{:S(2)}, u32[]{:S(2)}) async-start(bf16[64,8,512]{2,1,0:T(8,128)(2,1)} %bitcast.33), calls=%async_computation.3 | async-start | bytes 1048576 | tf_op jit(solution)/shard_map/all_to_all | solution.py:197
  174.8 1.4 copy-start.5

commit v2 on v1

v2 whole, which is shorter than its diff:
```python
import jax
import jax.numpy as jnp
from jax import lax
from jax.experimental import pallas as pl
from jax.experimental.pallas import tpu as pltpu
from jax.sharding import Mesh
from jax.sharding import PartitionSpec as P

clip_low = 0.8
clip_high = 1.25

bf16 = jnp.bfloat16
f32 = jnp.float32

NN = (((1,), (0,)), ((), ()))
NT = (((1,), (1,)), ((), ()))
TN = (((0,), (0,)), ((), ()))

QUAD = 4
SLOTS = 2
TILE = 8
LANE = 128


def mm(a, b, dims):
    return lax.dot_general(a, b, dims, preferred_element_type=f32)


def call(body, outs, flops, nbytes, **more):
    return pl.pallas_call(
        body,
        out_shape=outs,
        cost_estimate=pl.CostEstimate(flops=flops, bytes_accessed=nbytes, transcendentals=0),
        compiler_params=pltpu.CompilerParams(vmem_limit_bytes=24 * 1024 * 1024),
        **more,
    )


def me():
    return lax.axis_index("xh") * 2 + lax.axis_index("core")


def pieces(x):
    first = x.astype(bf16)
    rest = x - first.astype(f32)
    second = rest.astype(bf16)
    third = (rest - second.astype(f32)).astype(bf16)
    return jnp.concatenate([first, second, third], axis=0)


def pack_kernel(
    tokens_ref, cot_ref, probs_ref, ids_ref, seq_ref, ratios_ref, send_ref, table_ref, rows_ref
):
    count, width = tokens_ref.shape
    routes = ids_ref.shape[0]
    peers = send_ref.shape[0] // TILE
    experts = peers // QUAD
    down = lax.broadcasted_iota(jnp.int32, (count, count), 0)
    across = lax.broadcasted_iota(jnp.int32, (count, count), 1)

    def column(row):
        return jnp.sum(jnp.where(down == across, row, 0.0), axis=1, keepdims=True)

    labels = lax.broadcasted_iota(jnp.int32, (count, ratios_ref.shape[1]), 1).astype(f32)
    same = labels == column(seq_ref[...].astype(f32))
    picked = jnp.sum(jnp.where(same, ratios_ref[...], 0.0), axis=1, keepdims=True)
    weights = jnp.clip(picked, clip_low, clip_high)
    ids = ids_ref[...].astype(f32)
    peer = lax.broadcasted_iota(jnp.int32, (count, peers), 1)
    owner = lax.rem(peer, experts).astype(f32)
    first_slot = (lax.div(peer, experts) * SLOTS).astype(f32)
    member = jnp.zeros((count, peers), f32)
    prob_at = jnp.zeros((count, peers), f32)
    for k in range(routes):
        named = column(ids[k : k + 1, :]) == owner
        member = jnp.where(named, 1.0, member)
        prob_at = jnp.where(named, column(probs_ref[k : k + 1, :]), prob_at)
    scale_at = prob_at * weights
    lower = jnp.where(down > across, 1.0, 0.0).astype(bf16)
    before = mm(lower, member.astype(bf16), NN)
    cot = cot_ref[...]
    cots = jnp.concatenate([cot, cot, cot], axis=0)
    for s in range(SLOTS):
        here = (member > 0.0) & (before == first_slot + s)
        table = jnp.where(here, 1.0, 0.0).astype(bf16)
        table_ref[s, 0 : 3 * count, :] = pieces(jnp.where(here, prob_at, 0.0))
        table_ref[s, 3 * count : 4 * count, :] = table
        inputs = mm(table, tokens_ref[...], TN)
        seeds = mm(pieces(jnp.where(here, scale_at, 0.0)), cots, TN)
        for c in range(2):
            at = slice(c * LANE, (c + 1) * LANE)
            rows_ref[pl.ds(s * 4 + c, peers, stride=TILE), :] = inputs[:, at]
            rows_ref[pl.ds(s * 4 + 2 + c, peers, stride=TILE), :] = seeds[:, at]
    send_ref[...] = rows_ref[...].astype(bf16)


def gather_kernel(gate_ref, up_ref, down_ref, out_ref):
    width = gate_ref.shape[0]
    out_ref[0:width, :] = gate_ref[...]
    out_ref[width : 2 * width, :] = up_ref[...]
    out_ref[2 * width : 3 * width, :] = down_ref[...].T


def partial_kernel(came_ref, w0, w1, w2, w3, x_ref, out_ref, rows_ref, stage_ref):
    peers = came_ref.shape[0] // TILE
    blocks = peers // QUAD
    hidden = w0.shape[1]
    width = w0.shape[0] // 3
    wide = QUAD * width
    rows_ref[...] = came_ref[...].astype(f32)
    for j in range(TILE):
        stage_ref[j] = rows_ref[pl.ds(j, peers, stride=TILE), :].astype(bf16)
    mine = me()
    for k in range(QUAD):
        at = pl.ds(pl.multiple_of((mine ^ k) * blocks, blocks), blocks)
        for s in range(SLOTS):
            for c in range(4):
                column = (c // 2) * wide + k * width + (c % 2) * LANE
                x_ref[s * blocks : (s + 1) * blocks, column : column + LANE] = stage_ref[
                    s * 4 + c, at, :
                ]
    for part in range(3):
        total = jnp.zeros((SLOTS * blocks, hidden), f32)
        for k, w in enumerate((w0, w1, w2, w3)):
            column = (part // 2) * wide + k * width
            total = total + mm(
                x_ref[:, column : column + width], w[part * width : (part + 1) * width, :], NN
            )
        out_ref[:, part * hidden : (part + 1) * hidden] = total.astype(bf16)


def middle_kernel(parts_ref, out_ref):
    groups, rows, wide = parts_ref.shape
    hidden = wide // 3
    total = parts_ref[0].astype(f32)
    for g in range(1, groups):
        total = total + parts_ref[g].astype(f32)
    gate_sum = total[:, 0:hidden]
    up_sum = total[:, hidden : 2 * hidden]
    hidden_cot = total[:, 2 * hidden : 3 * hidden]
    sigmoid = 1.0 / (1.0 + jnp.exp(-gate_sum))
    active = gate_sum * sigmoid
    slopes = sigmoid * (1.0 + gate_sum * (1.0 - sigmoid))
    inner = (active * up_sum).astype(bf16)
    gate_cot = (hidden_cot * up_sum * slopes).astype(bf16)
    up_cot = (hidden_cot * active).astype(bf16)
    for g in range(groups):
        out_ref[g, :, 0:hidden] = inner
        out_ref[g, :, hidden : 2 * hidden] = gate_cot
        out_ref[g, :, 2 * hidden : 3 * hidden] = up_cot


def back_kernel(hgu_ref, w0, w1, w2, w3, send_ref, stage_ref, rows_ref):
    hidden = w0.shape[1]
    width = w0.shape[0] // 3
    blocks = hgu_ref.shape[0] // SLOTS
    peers = QUAD * blocks
    mine = me()
    inner = hgu_ref[:, 0:hidden]
    gate_cot = hgu_ref[:, hidden : 2 * hidden]
    up_cot = hgu_ref[:, 2 * hidden : 3 * hidden]
    for k, w in enumerate((w0, w1, w2, w3)):
        out = mm(inner, w[2 * width : 3 * width, :], NT)
        back = mm(gate_cot, w[0:width, :], NT) + mm(up_cot, w[width : 2 * width, :], NT)
        at = pl.ds(pl.multiple_of((mine ^ k) * blocks, blocks), blocks)
        for s in range(SLOTS):
            rows = slice(s * blocks, (s + 1) * blocks)
            for c in range(2):
                lanes = slice(c * LANE, (c + 1) * LANE)
                stage_ref[s * 4 + c, at, :] = out[rows, lanes]
                stage_ref[s * 4 + 2 + c, at, :] = back[rows, lanes]
    for j in range(TILE):
        rows_ref[pl.ds(j, peers, stride=TILE), :] = stage_ref[j]
    send_ref[...] = rows_ref[...].astype(bf16)


def grads_kernel(x_ref, hgu_ref, keep_ref, send_ref):
    hidden = hgu_ref.shape[1] // 3
    width = keep_ref.shape[1] // 3
    wide = QUAD * width
    for k in range(QUAD):
        out_ref = send_ref if k % 2 else keep_ref
        for part, (column, factor) in enumerate(((0, 1), (0, 2), (1, 0))):
            start = column * wide + k * width
            out_ref[k // 2, part * width : (part + 1) * width, :] = mm(
                x_ref[:, start : start + width],
                hgu_ref[:, factor * hidden : (factor + 1) * hidden],
                TN,
            ).astype(bf16)


def first_sum_kernel(keep_ref, came_ref, own_ref, other_ref):
    own_ref[...] = (keep_ref[0].astype(f32) + came_ref[0].astype(f32)).astype(bf16)
    other_ref[...] = (keep_ref[1].astype(f32) + came_ref[1].astype(f32)).astype(bf16)


def last_sum_kernel(own_ref, came_ref, gate_ref, up_ref, down_ref):
    width = gate_ref.shape[0]

    def total(part):
        at = slice(part * width, (part + 1) * width)
        return (own_ref[at, :].astype(f32) + came_ref[at, :].astype(f32)).astype(bf16)

    gate_ref[...] = total(0)
    up_ref[...] = total(1)
    down_ref[...] = total(2).T


def combine_kernel(table_ref, came_ref, out_ref, grad_ref, rows_ref):
    count, width = out_ref.shape
    peers = came_ref.shape[0] // TILE
    rows_ref[...] = came_ref[...].astype(f32)

    def picked(s, c):
        return jnp.concatenate(
            [rows_ref[pl.ds(s * 4 + c + i, peers, stride=TILE), :] for i in range(2)], axis=1
        ).astype(bf16)

    parts = jnp.zeros((3 * count, width), f32)
    grad = jnp.zeros((count, width), f32)
    for s in range(SLOTS):
        parts = parts + mm(table_ref[s, 0 : 3 * count, :], picked(s, 0), NN)
        grad = grad + mm(table_ref[s, 3 * count : 4 * count, :], picked(s, 2), NN)
    out_ref[...] = (
        parts[0:count] + parts[count : 2 * count] + parts[2 * count : 3 * count]
    ).astype(bf16)
    grad_ref[...] = grad.astype(bf16)


def local(
    tokens, cotangent, route_probs, expert_ids, seq_ids, ratios, gate_weight, up_weight, down_weight
):
    count, width = tokens.shape
    hidden = gate_weight.shape[2]
    sources = lax.axis_size("replica")
    groups = lax.axis_size("y")
    peers = QUAD * sources
    rows = SLOTS * sources
    shape = jax.ShapeDtypeStruct
    message = shape((peers * TILE, LANE), bf16)
    everyone = ("xh", "core", "replica")
    flip = [(0, 1), (1, 0)]
    product = 2 * rows * QUAD * width * hidden
    weight_bytes = 2 * 3 * QUAD * width * hidden

    def spread(x, axis):
        return lax.all_to_all(x, axis, split_axis=0, concat_axis=0, tiled=True)

    def messages(x):
        return spread(x.reshape(peers, TILE, LANE), everyone).reshape(peers * TILE, LANE)

    send, table = call(
        pack_kernel,
        (message, shape((SLOTS, 4 * count, peers), bf16)),
        16 * peers * count * width,
        4 * peers * TILE * LANE,
        scratch_shapes=[pltpu.VMEM((peers * TILE, LANE), f32)],
    )(
        tokens,
        cotangent,
        route_probs.T,
        expert_ids.T,
        seq_ids.reshape(1, count),
        ratios.reshape(1, -1),
    )
    came = messages(send)

    w0 = call(gather_kernel, shape((3 * width, hidden), bf16), 0, 12 * width * hidden)(
        gate_weight[0], up_weight[0], down_weight[0]
    )
    w2 = lax.ppermute(w0, "xh", flip)
    w1 = lax.ppermute(w0, "core", flip)
    w3 = lax.ppermute(w2, "core", flip)

    x, partial = call(
        partial_kernel,
        (shape((rows, 2 * QUAD * width), bf16), shape((rows, 3 * hidden), bf16)),
        3 * product,
        weight_bytes,
        scratch_shapes=[
            pltpu.VMEM((peers * TILE, LANE), f32),
            pltpu.VMEM((TILE, peers, LANE), bf16),
        ],
    )(came, w0, w1, w2, w3)
    parts = spread(partial.reshape(groups, rows // groups, 3 * hidden), "y")
    copies = call(
        middle_kernel,
        shape((groups, rows // groups, 3 * hidden), bf16),
        20 * rows * 3 * hidden,
        4 * rows * 3 * hidden,
    )(parts)
    hgu = spread(copies, "y").reshape(rows, 3 * hidden)
    sent_back = call(
        back_kernel,
        message,
        3 * product,
        weight_bytes,
        scratch_shapes=[
            pltpu.VMEM((TILE, peers, LANE), f32),
            pltpu.VMEM((peers * TILE, LANE), f32),
        ],
    )(hgu, w0, w1, w2, w3)

    pair = shape((2, 3 * width, hidden), bf16)
    one = shape((3 * width, hidden), bf16)
    x, hgu, sent_back = lax.optimization_barrier((x, hgu, sent_back))
    returned = messages(sent_back)
    keep, give = call(grads_kernel, (pair, pair), 3 * product, weight_bytes)(x, hgu)
    got = lax.ppermute(give, "core", flip)
    own, other = call(first_sum_kernel, (one, one), 6 * width * hidden, 2 * weight_bytes)(keep, got)
    theirs = lax.ppermute(other, "xh", flip)
    grads = call(
        last_sum_kernel,
        (
            shape((width, hidden), bf16),
            shape((width, hidden), bf16),
            shape((hidden, width), bf16),
        ),
        3 * width * hidden,
        weight_bytes,
    )(own, theirs)
    layer_out, grad_tokens = call(
        combine_kernel,
        (shape((count, width), bf16), shape((count, width), bf16)),
        16000 * peers * count * width,
        4 * peers * TILE * LANE,
        scratch_shapes=[pltpu.VMEM((peers * TILE, LANE), f32)],
    )(table, returned)
    return (layer_out, grad_tokens) + tuple(g[None] for g in grads)


def solution(mesh):
    groups = mesh.shape["expert"] // QUAD
    quads = Mesh(
        mesh.devices.reshape(groups, 2, 2, mesh.shape["replica"]), ("y", "xh", "core", "replica")
    )
    expert = ("y", "xh", "core")
    return jax.shard_map(
        local,
        mesh=quads,
        in_specs=(
            P("replica", expert),
            P("replica", expert),
            P("replica", None),
            P("replica", None),
            P("replica"),
            P(),
            P("replica", expert, None),
            P("replica", expert, None),
            P("replica", None, expert),
        ),
        out_specs=(
            P("replica", expert),
            P("replica", expert),
            P("replica", expert, None),
            P("replica", expert, None),
            P("replica", None, expert),
        ),
        check_vma=False,
    )
```

time: 236 us -> 231 us (0.979); the launches traced: 232 us -> 230 us
  blocking collectives: 139 us -> 27 us
  starting transfers between devices: 19.7 us -> 81.8 us
  waiting for transfers between devices: 57.9 us -> 90.6 us
  local copies, waits for them, and re-layouts: 8.24 us -> 16.1 us
  Pallas kernels: 6.29 us -> 13.8 us
    all_to_all x3 -> x2, blocking collectives: 139 us -> 27 us  [spread(): return lax.all_to_all(x, axis, split_axis=0, concat_axis=0, tiled=True)]
    all_to_all x1 -> x2, starting transfers between devices: 10.4 us -> 62.7 us  [spread(): return lax.all_to_all(x, axis, split_axis=0, concat_axis=0, tiled=True)]
    ppermute x2 -> x5, waiting for transfers between devices: 4.85 us -> 43.4 us  [the longest x1 36.3 us: local(): w2 = lax.ppermute(w0, 'xh', flip)]
    ppermute x2 -> x5, starting transfers between devices: 9.25 us -> 19.2 us  [the longest x1 5.64 us: local(): w2 = lax.ppermute(w0, 'xh', flip)]
    unnamed x24 -> x40, local copies, waits for them, and re-layouts: 8.24 us -> 16.1 us
    pallas_call x8, Pallas kernels: 5.46 us -> 11.8 us  [the longest x1 2.53 us: local(): call(back_kernel, message, 3 * product, weight_bytes, scratch_shapes=[plt...]
    all_to_all x1 -> x2, waiting for transfers between devices: 53 us -> 47.2 us  [spread(): return lax.all_to_all(x, axis, split_axis=0, concat_axis=0, tiled=True)]
  transfers between devices with their start and end apart: 3 -> 7, of which waited for: 3 -> 5; matrix products, arithmetic and copies ran while one was open for 0% -> 0% of each run, Pallas kernels for 1% -> 3%
where the time goes in v2:
time: 231 us; the launch traced here: 230 us
  waiting for transfers between devices  90.6 us (39%)
  starting transfers between devices  81.8 us (35%)
  blocking collectives  27 us (12%)
  local copies, waits for them, and re-layouts  16.1 us (7%)
  Pallas kernels  13.8 us (6%)
    all_to_all x2, starting transfers between devices, spread(): return lax.all_to_all(x, axis, split_axis=0, concat_axis=0, tiled=True)  62.7 us
    all_to_all x2, waiting for transfers between devices, spread(): return lax.all_to_all(x, axis, split_axis=0, concat_axis=0, tiled=True)  47.2 us
    ppermute x1, waiting for transfers between devices, local(): w2 = lax.ppermute(w0, 'xh', flip)  36.3 us
    all_to_all x2, blocking collectives, spread(): return lax.all_to_all(x, axis, split_axis=0, concat_axis=0, tiled=True)  27 us
    unnamed x40, local copies, waits for them, and re-layouts  16.1 us
    ppermute x1, starting transfers between devices, local(): w2 = lax.ppermute(w0, 'xh', flip)  5.64 us
    ppermute x1, waiting for transfers between devices, local(): got = lax.ppermute(give, 'core', flip)  5.26 us
  transfers between devices with their start and end apart: 7, of which 5 were waited for; matrix products, arithmetic and copies ran while one was open for 0% of the time, Pallas kernels for 3%

profile of v2, /device:TPU:1, one launch (start us, length us, event | category | flops | bytes accessed | tf_op | source)
XLA Modules:
  0.0 230.1 jit_solution(17873465761709821765)
XLA Ops:
  4.8 1.4 shard_map.128
  6.2 36.5 %all-to-all-start = ((bf16[256,8,128]{2,1,0:T(8,128)(2,1)}), bf16[256,8,128]{2,1,0:T(8,128)(2,1)}, u32[]{:S(2)}, u32[]{:S(2)}) async-start(bf16[256,8,128]{2,1,0:T(8,128)(2,1)} %bitcast.4), calls=%async_computation | async-start | bytes 1048576 | tf_op jit(solution)/shard_map/all_to_all | solution.py:247
  46.1 5.6 %collective-permute-start.1 = (bf16[768,1024]{1,0:T(8,128)(2,1)S(1)}, bf16[768,1024]{1,0:T(8,128)(2,1)S(1)}, u32[]{:S(2)}, u32[]{:S(2)}) collective-permute-start(bf16[768,1024]{1,0:T(8,128)(2,1)S(1)} %shard_map.129.w0), channel_id=1, source_target_pairs={{0,128},{128,0},{1,129},{129,1},{2,130},{130,2},{3,131},{131,3},{4... | collective-permute-start | bytes 4718600 | tf_op jit(solution)/shard_map/ppermute | solution.py:271
  51.7 2.1 collective-permute-start
  53.9 36.3 %collective-permute-done.1.w2 = bf16[768,1024]{1,0:T(8,128)(2,1)S(1)} collective-permute-done((bf16[768,1024]{1,0:T(8,128)(2,1)S(1)}, bf16[768,1024]{1,0:T(8,128)(2,1)S(1)}, u32[]{:S(2)}, u32[]{:S(2)}) %collective-permute-start.1) | collective-permute-done | bytes 1572896 | tf_op jit(solution)/shard_map/ppermute | solution.py:271
  90.1 3.5 %collective-permute-start.2 = (bf16[768,1024]{1,0:T(8,128)(2,1)S(1)}, bf16[768,1024]{1,0:T(8,128)(2,1)S(1)}, u32[]{:S(2)}, u32[]{:S(2)}) collective-permute-start(bf16[768,1024]{1,0:T(8,128)(2,1)S(1)} %collective-permute-done.1.w2), channel_id=1, source_target_pairs={{0,64},{64,0},{1,65},{65,1},{2,66},{66,2},{3,67},{67,3},{4,68},{68... | collective-permute-start | bytes 4718600 | tf_op jit(solution)/shard_map/ppermute | solution.py:273
  93.6 1.2 copy-done
  94.8 1.8 collective-permute-done.2.w3
  97.8 5.5 %all-to-all-done = bf16[256,8,128]{2,1,0:T(8,128)(2,1)} async-done(((bf16[256,8,128]{2,1,0:T(8,128)(2,1)}), bf16[256,8,128]{2,1,0:T(8,128)(2,1)}, u32[]{:S(2)}, u32[]{:S(2)}) %all-to-all-start) | async-done | bytes 524320 | tf_op jit(solution)/shard_map/all_to_all | solution.py:247
  103.3 1.4 copy-done.1
  104.8 1.4 copy-done.4
  106.2 2.2 shard_map.130
  109.2 14.7 %all_to_all.20.parts_ref = bf16[4,32,3072]{2,1,0:T(8,128)(2,1)S(1)} all-to-all(bf16[4,32,3072]{2,1,0:T(8,128)(2,1)S(1)} %bitcast.19), channel_id=1, replica_groups=mesh['y'=4,'xh'=2,'core'=2,'replica'=64] {'y'}, dimensions={0} | all-to-all | bytes 1572864 | tf_op jit(solution)/shard_map/all_to_all | solution.py:247
  124.0 12.3 %all_to_all.21 = bf16[4,32,3072]{2,1,0:T(8,128)(2,1)S(1)} all-to-all(bf16[4,32,3072]{2,1,0:T(8,128)(2,1)S(1)} %shard_map.131), channel_id=1, replica_groups=mesh['y'=4,'xh'=2,'core'=2,'replica'=64] {'y'}, dimensions={0} | all-to-all | bytes 1572864 | tf_op jit(solution)/shard_map/all_to_all | solution.py:247
  136.4 2.5 %shard_map.132 = bf16[2048,128]{1,0:T(8,128)(2,1)S(1)} custom-call(bf16[128,3072]{1,0:T(8,128)(2,1)S(1)} %bitcast.16, bf16[768,1024]{1,0:T(8,128)(2,1)S(1)} %shard_map.129.w0, bf16[768,1024]{1,0:T(8,128)(2,1)S(1)} %copy-done.2, bf16[768,1024]{1,0:T(8,128)(2,1)S(1)} %collective-permute-done.1.w2, bf16[768,1024]{1,0:T(8,128)(2,1)S(1)} %copy-done.5), custom_call_target="tpu_custom_call" | custom-call | flops 805306368 | bytes 6291456 | tf_op jit(solution)/shard_map/pallas_call | solution.py:293
  139.7 26.2 %all-to-all-start.3 = ((bf16[256,8,128]{2,1,0:T(8,128)(2,1)}), bf16[256,8,128]{2,1,0:T(8,128)(2,1)}, u32[]{:S(2)}, u32[]{:S(2)}) async-start(bf16[256,8,128]{2,1,0:T(8,128)(2,1)} %bitcast.18), calls=%async_computation.3 | async-start | bytes 1048576 | tf_op jit(solution)/shard_map/all_to_all | solution.py:247
  168.1 1.8 shard_map.134
  169.9 3.4 %collective-permute-start.3 = (bf16[2,768,1024]{2,1,0:T(8,128)(2,1)S(1)}, bf16[2,768,1024]{2,1,0:T(8,128)(2,1)S(1)}, u32[]{:S(2)}, u32[]{:S(2)}) collective-permute-start(bf16[2,768,1024]{2,1,0:T(8,128)(2,1)S(1)} %get-tuple-element.31), channel_id=1, source_target_pairs={{0,64},{64,0},{1,65},{65,1},{2,66},{66,2},{3,67},{67,3},{4,68},{68... | collective-permute-start | bytes 9437192 | tf_op jit(solution)/shard_map/ppermute | solution.py:309
  173.3 5.3 %collective-permute-done.3.came_ref = bf16[2,768,1024]{2,1,0:T(8,128)(2,1)S(1)} collective-permute-done((bf16[2,768,1024]{2,1,0:T(8,128)(2,1)S(1)}, bf16[2,768,1024]{2,1,0:T(8,128)(2,1)S(1)}, u32[]{:S(2)}, u32[]{:S(2)}) %collective-permute-start.3) | collective-permute-done | bytes 3145760 | tf_op jit(solution)/shard_map/ppermute | solution.py:309
  178.6 1.8 shard_map.135
  180.4 4.5 %collective-permute-start.4 = (bf16[768,1024]{1,0:T(8,128)(2,1)}, bf16[768,1024]{1,0:T(8,128)(2,1)S(1)}, u32[]{:S(2)}, u32[]{:S(2)}) collective-permute-start(bf16[768,1024]{1,0:T(8,128)(2,1)} %get-tuple-element.33), channel_id=1, source_target_pairs={{0,128},{128,0},{1,129},{129,1},{2,130},{130,2},{3,131},{131,3},{4... | collective-permute-start | bytes 4718600 | tf_op jit(solution)/shard_map/ppermute | solution.py:311
  184.9 41.6 %all-to-all-done.3 = bf16[256,8,128]{2,1,0:T(8,128)(2,1)} async-done(((bf16[256,8,128]{2,1,0:T(8,128)(2,1)}), bf16[256,8,128]{2,1,0:T(8,128)(2,1)}, u32[]{:S(2)}, u32[]{:S(2)}) %all-to-all-start.3) | async-done | bytes 524320 | tf_op jit(solution)/shard_map/all_to_all | solution.py:247
  226.5 2.0 shard_map.133
  228.5 1.5 shard_map.136
  (41 shorter events, 12.5 us)
Async XLA Ops:
  0.6 0.7 copy-start.14
  1.4 0.7 copy-start.15
  2.1 0.7 copy-start.16
  6.2 97.1 %all-to-all-start = ((bf16[256,8,128]{2,1,0:T(8,128)(2,1)}), bf16[256,8,128]{2,1,0:T(8,128)(2,1)}, u32[]{:S(2)}, u32[]{:S(2)}) async-start(bf16[256,8,128]{2,1,0:T(8,128)(2,1)} %bitcast.4), calls=%async_computation | async-start | bytes 1048576 | tf_op jit(solution)/shard_map/all_to_all | solution.py:247
  42.7 1.0 copy-start.9
  43.8 1.0 copy-start.10
  44.8 1.0 copy-start.11
  46.1 44.1 %collective-permute-start.1 = (bf16[768,1024]{1,0:T(8,128)(2,1)S(1)}, bf16[768,1024]{1,0:T(8,128)(2,1)S(1)}, u32[]{:S(2)}, u32[]{:S(2)}) collective-permute-start(bf16[768,1024]{1,0:T(8,128)(2,1)S(1)} %shard_map.129.w0), channel_id=1, source_target_pairs={{0,128},{128,0},{1,129},{129,1},{2,130},{130,2},{3,131},{131,3},{4... | collective-permute-start | bytes 4718600 | tf_op jit(solution)/shard_map/ppermute | solution.py:271
  51.7 41.9 %collective-permute-start = (bf16[768,1024]{1,0:T(8,128)(2,1)S(1)}, bf16[768,1024]{1,0:T(8,128)(2,1)S(1)}, u32[]{:S(2)}, u32[]{:S(2)}) collective-permute-start(bf16[768,1024]{1,0:T(8,128)(2,1)S(1)} %shard_map.129.w0), channel_id=1, source_target_pairs={{0,64},{64,0},{1,65},{65,1},{2,66},{66,2},{3,67},{67,3},{4,68},{68... | collective-permute-start | bytes 4718600 | tf_op jit(solution)/shard_map/ppermute | solution.py:272
  90.1 6.5 %collective-permute-start.2 = (bf16[768,1024]{1,0:T(8,128)(2,1)S(1)}, bf16[768,1024]{1,0:T(8,128)(2,1)S(1)}, u32[]{:S(2)}, u32[]{:S(2)}) collective-permute-start(bf16[768,1024]{1,0:T(8,128)(2,1)S(1)} %collective-permute-done.1.w2), channel_id=1, source_target_pairs={{0,64},{64,0},{1,65},{65,1},{2,66},{66,2},{3,67},{67,3},{4,68},{68... | collective-permute-start | bytes 4718600 | tf_op jit(solution)/shard_map/ppermute | solution.py:273
  93.6 1.2 copy-start
  96.6 1.2 copy-start.3
  103.3 1.4 copy-start.1
  104.7 1.4 copy-start.4
  108.4 0.8 copy-start.12
  123.9 12.5 %copy-start.2 = (bf16[768,1024]{1,0:T(8,128)(2,1)S(1)}, bf16[768,1024]{1,0:T(8,128)(2,1)}, u32[]{:S(2)}) copy-start(bf16[768,1024]{1,0:T(8,128)(2,1)} %copy-done) | copy-start | bytes 4718596
  123.9 12.5 %copy-start.5 = (bf16[768,1024]{1,0:T(8,128)(2,1)S(1)}, bf16[768,1024]{1,0:T(8,128)(2,1)}, u32[]{:S(2)}) copy-start(bf16[768,1024]{1,0:T(8,128)(2,1)} %copy-done.3) | copy-start | bytes 4718596
  136.3 2.6 %copy-start.6 = (bf16[4,32,3072]{2,1,0:T(8,128)(2,1)}, bf16[4,32,3072]{2,1,0:T(8,128)(2,1)S(1)}, u32[]{:S(2)}) copy-start(bf16[4,32,3072]{2,1,0:T(8,128)(2,1)S(1)} %all_to_all.21) | copy-start | bytes 2359300
  138.9 0.8 copy-start.8
  139.7 86.8 %all-to-all-start.3 = ((bf16[256,8,128]{2,1,0:T(8,128)(2,1)}), bf16[256,8,128]{2,1,0:T(8,128)(2,1)}, u32[]{:S(2)}, u32[]{:S(2)}) async-start(bf16[256,8,128]{2,1,0:T(8,128)(2,1)} %bitcast.18), calls=%async_computation.3 | async-start | bytes 1048576 | tf_op jit(solution)/shard_map/all_to_all | solution.py:247
  165.9 1.1 copy-start.7
  167.0 1.0 copy-start.13
  169.9 8.7 %collective-permute-start.3 = (bf16[2,768,1024]{2,1,0:T(8,128)(2,1)S(1)}, bf16[2,768,1024]{2,1,0:T(8,128)(2,1)S(1)}, u32[]{:S(2)}, u32[]{:S(2)}) collective-permute-start(bf16[2,768,1024]{2,1,0:T(8,128)(2,1)S(1)} %get-tuple-element.31), channel_id=1, source_target_pairs={{0,64},{64,0},{1,65},{65,1},{2,66},{66,2},{3,67},{67,3},{4,68},{68... | collective-permute-start | bytes 9437192 | tf_op jit(solution)/shard_map/ppermute | solution.py:309
  180.4 48.1 %collective-permute-start.4 = (bf16[768,1024]{1,0:T(8,128)(2,1)}, bf16[768,1024]{1,0:T(8,128)(2,1)S(1)}, u32[]{:S(2)}, u32[]{:S(2)}) collective-permute-start(bf16[768,1024]{1,0:T(8,128)(2,1)} %get-tuple-element.33), channel_id=1, source_target_pairs={{0,128},{128,0},{1,129},{129,1},{2,130},{130,2},{3,131},{131,3},{4... | collective-permute-start | bytes 4718600 | tf_op jit(solution)/shard_map/ppermute | solution.py:311
  (3 other events, 2.0 us)

commit v3 on v2

--- a/solution.py
+++ b/solution.py
@@ -26,18 +26,18 @@
     return lax.dot_general(a, b, dims, preferred_element_type=f32)
 
 
-def call(body, outs, flops, nbytes, **more):
+def call(body, outs, flops, nbytes, room=24, **more):
     return pl.pallas_call(
         body,
         out_shape=outs,
         cost_estimate=pl.CostEstimate(flops=flops, bytes_accessed=nbytes, transcendentals=0),
-        compiler_params=pltpu.CompilerParams(vmem_limit_bytes=24 * 1024 * 1024),
+        compiler_params=pltpu.CompilerParams(vmem_limit_bytes=room * 1024 * 1024),
         **more,
     )
 
 
 def me():
-    return lax.axis_index("xh") * 2 + lax.axis_index("core")
+    return lax.axis_index("yl") * 2 + lax.axis_index("core")
 
 
 def pieces(x):
@@ -48,9 +48,14 @@
     return jnp.concatenate([first, second, third], axis=0)
 
 
-def pack_kernel(
-    tokens_ref, cot_ref, probs_ref, ids_ref, seq_ref, ratios_ref, send_ref, table_ref, rows_ref
-):
+def pack_kernel(*refs):
+    arrays, (send_ref, table_ref, rows_ref), held, sem = refs[:6], refs[6:9], refs[9:15], refs[15]
+    copies = [pltpu.make_async_copy(a, b, sem.at[i]) for i, (a, b) in enumerate(zip(arrays, held))]
+    for copy in copies:
+        copy.start()
+    for copy in copies:
+        copy.wait()
+    tokens_ref, cot_ref, probs_ref, ids_ref, seq_ref, ratios_ref = held
     count, width = tokens_ref.shape
     routes = ids_ref.shape[0]
     peers = send_ref.shape[0] // TILE
@@ -233,12 +238,13 @@
     count, width = tokens.shape
     hidden = gate_weight.shape[2]
     sources = lax.axis_size("replica")
-    groups = lax.axis_size("y")
+    others = ("xh", "yh")
+    groups = lax.axis_size("xh") * lax.axis_size("yh")
     peers = QUAD * sources
     rows = SLOTS * sources
     shape = jax.ShapeDtypeStruct
     message = shape((peers * TILE, LANE), bf16)
-    everyone = ("xh", "core", "replica")
+    everyone = ("yl", "core", "replica")
     flip = [(0, 1), (1, 0)]
     product = 2 * rows * QUAD * width * hidden
     weight_bytes = 2 * 3 * QUAD * width * hidden
@@ -249,13 +255,7 @@
     def messages(x):
         return spread(x.reshape(peers, TILE, LANE), everyone).reshape(peers * TILE, LANE)
 
-    send, table = call(
-        pack_kernel,
-        (message, shape((SLOTS, 4 * count, peers), bf16)),
-        16 * peers * count * width,
-        4 * peers * TILE * LANE,
-        scratch_shapes=[pltpu.VMEM((peers * TILE, LANE), f32)],
-    )(
+    arrays = (
         tokens,
         cotangent,
         route_probs.T,
@@ -263,12 +263,23 @@
         seq_ids.reshape(1, count),
         ratios.reshape(1, -1),
     )
+    send, table = call(
+        pack_kernel,
+        (message, shape((SLOTS, 4 * count, peers), bf16)),
+        16 * peers * count * width,
+        4 * peers * TILE * LANE,
+        60,
+        in_specs=[pl.BlockSpec(memory_space=pl.ANY)] * len(arrays),
+        scratch_shapes=[pltpu.VMEM((peers * TILE, LANE), f32)]
+        + [pltpu.VMEM(a.shape, a.dtype) for a in arrays]
+        + [pltpu.SemaphoreType.DMA((len(arrays),))],
+    )(*arrays)
     came = messages(send)
 
     w0 = call(gather_kernel, shape((3 * width, hidden), bf16), 0, 12 * width * hidden)(
         gate_weight[0], up_weight[0], down_weight[0]
     )
-    w2 = lax.ppermute(w0, "xh", flip)
+    w2 = lax.ppermute(w0, "yl", flip)
     w1 = lax.ppermute(w0, "core", flip)
     w3 = lax.ppermute(w2, "core", flip)
 
@@ -282,14 +293,14 @@
             pltpu.VMEM((TILE, peers, LANE), bf16),
         ],
     )(came, w0, w1, w2, w3)
-    parts = spread(partial.reshape(groups, rows // groups, 3 * hidden), "y")
+    parts = spread(partial.reshape(groups, rows // groups, 3 * hidden), others)
     copies = call(
         middle_kernel,
         shape((groups, rows // groups, 3 * hidden), bf16),
         20 * rows * 3 * hidden,
         4 * rows * 3 * hidden,
     )(parts)
-    hgu = spread(copies, "y").reshape(rows, 3 * hidden)
+    hgu = spread(copies, others).reshape(rows, 3 * hidden)
     sent_back = call(
         back_kernel,
         message,
@@ -303,12 +314,11 @@
 
     pair = shape((2, 3 * width, hidden), bf16)
     one = shape((3 * width, hidden), bf16)
-    x, hgu, sent_back = lax.optimization_barrier((x, hgu, sent_back))
     returned = messages(sent_back)
     keep, give = call(grads_kernel, (pair, pair), 3 * product, weight_bytes)(x, hgu)
     got = lax.ppermute(give, "core", flip)
     own, other = call(first_sum_kernel, (one, one), 6 * width * hidden, 2 * weight_bytes)(keep, got)
-    theirs = lax.ppermute(other, "xh", flip)
+    theirs = lax.ppermute(other, "yl", flip)
     grads = call(
         last_sum_kernel,
         (
@@ -330,11 +340,10 @@
 
 
 def solution(mesh):
-    groups = mesh.shape["expert"] // QUAD
-    quads = Mesh(
-        mesh.devices.reshape(groups, 2, 2, mesh.shape["replica"]), ("y", "xh", "core", "replica")
-    )
-    expert = ("y", "xh", "core")
+    axes = ("yh", "yl", "xh", "core")
+    shape = (mesh.shape["expert"] // 8, 2, 2, 2, mesh.shape["replica"])
+    quads = Mesh(mesh.devices.reshape(shape), axes + ("replica",))
+    expert = axes
     return jax.shard_map(
         local,
         mesh=quads,

time: 231 us -> 230 us (level)
  starting transfers between devices: 81.8 us -> 75.6 us
  blocking collectives: 27 us -> 32.5 us
  local copies, waits for them, and re-layouts: 16.1 us -> 12 us
  waiting for transfers between devices: 90.6 us -> 93.6 us
    all_to_all x2, blocking collectives: 27 us -> 32.5 us  [spread(): return lax.all_to_all(x, axis, split_axis=0, concat_axis=0, tiled=True)]
    unnamed x40 -> x30, local copies, waits for them, and re-layouts: 16.1 us -> 12 us
    all_to_all x2, waiting for transfers between devices: 47.2 us -> 50.4 us  [spread(): return lax.all_to_all(x, axis, split_axis=0, concat_axis=0, tiled=True)]
    all_to_all x2, starting transfers between devices: 62.7 us -> 59.5 us  [spread(): return lax.all_to_all(x, axis, split_axis=0, concat_axis=0, tiled=True)]
    ppermute x2, starting transfers between devices: 10.1 us -> 7.1 us  [the longest x1 4.14 us: local(): w2 = lax.ppermute(w0, 'yl', flip)]
where the time goes in v3:
time: 230 us; the launch traced here: 229 us
  waiting for transfers between devices  93.6 us (41%)
  starting transfers between devices  75.6 us (33%)
  blocking collectives  32.5 us (14%)
  Pallas kernels  14.6 us (6%)
  local copies, waits for them, and re-layouts  12 us (5%)
    all_to_all x2, starting transfers between devices, spread(): return lax.all_to_all(x, axis, split_axis=0, concat_axis=0, tiled=True)  59.5 us
    all_to_all x2, waiting for transfers between devices, spread(): return lax.all_to_all(x, axis, split_axis=0, concat_axis=0, tiled=True)  50.4 us
    ppermute x1, waiting for transfers between devices, local(): w2 = lax.ppermute(w0, 'yl', flip)  36.1 us
    all_to_all x2, blocking collectives, spread(): return lax.all_to_all(x, axis, split_axis=0, concat_axis=0, tiled=True)  32.5 us
    unnamed x30, local copies, waits for them, and re-layouts  12 us
    ppermute x1, waiting for transfers between devices, local(): got = lax.ppermute(give, 'core', flip)  5.26 us
  transfers between devices with their start and end apart: 7, of which 5 were waited for; matrix products, arithmetic and copies ran while one was open for 0% of the time, Pallas kernels for 3%

profile of v3, /device:TPU:1, one launch (start us, length us, event | category | flops | bytes accessed | tf_op | source)
XLA Modules:
  0.0 229.1 jit_solution(13983603135459115781)
XLA Ops:
  0.6 2.3 shard_map.128
  2.9 36.0 %all-to-all-start = ((bf16[256,8,128]{2,1,0:T(8,128)(2,1)}), bf16[256,8,128]{2,1,0:T(8,128)(2,1)}, u32[]{:S(2)}, u32[]{:S(2)}) async-start(bf16[256,8,128]{2,1,0:T(8,128)(2,1)} %bitcast.23), calls=%async_computation | async-start | bytes 1048576 | tf_op jit(solution)/shard_map/all_to_all | solution.py:253
  42.2 4.1 %collective-permute-start.1 = (bf16[768,1024]{1,0:T(8,128)(2,1)S(1)}, bf16[768,1024]{1,0:T(8,128)(2,1)S(1)}, u32[]{:S(2)}, u32[]{:S(2)}) collective-permute-start(bf16[768,1024]{1,0:T(8,128)(2,1)S(1)} %shard_map.129.w0), channel_id=1, source_target_pairs={{0,256},{256,0},{1,257},{257,1},{2,258},{258,2},{3,259},{259,3},{4... | collective-permute-start | bytes 4718600 | tf_op jit(solution)/shard_map/ppermute | solution.py:282
  46.4 2.1 collective-permute-start
  48.5 36.1 %collective-permute-done.1.w2 = bf16[768,1024]{1,0:T(8,128)(2,1)S(1)} collective-permute-done((bf16[768,1024]{1,0:T(8,128)(2,1)S(1)}, bf16[768,1024]{1,0:T(8,128)(2,1)S(1)}, u32[]{:S(2)}, u32[]{:S(2)}) %collective-permute-start.1) | collective-permute-done | bytes 1572896 | tf_op jit(solution)/shard_map/ppermute | solution.py:282
  84.6 3.4 %collective-permute-start.2 = (bf16[768,1024]{1,0:T(8,128)(2,1)S(1)}, bf16[768,1024]{1,0:T(8,128)(2,1)S(1)}, u32[]{:S(2)}, u32[]{:S(2)}) collective-permute-start(bf16[768,1024]{1,0:T(8,128)(2,1)S(1)} %collective-permute-done.1.w2), channel_id=1, source_target_pairs={{0,64},{64,0},{1,65},{65,1},{2,66},{66,2},{3,67},{67,3},{4,68},{68... | collective-permute-start | bytes 4718600 | tf_op jit(solution)/shard_map/ppermute | solution.py:284
  88.1 1.2 copy-done
  89.3 1.8 collective-permute-done.2.w3
  92.2 7.3 %all-to-all-done = bf16[256,8,128]{2,1,0:T(8,128)(2,1)} async-done(((bf16[256,8,128]{2,1,0:T(8,128)(2,1)}), bf16[256,8,128]{2,1,0:T(8,128)(2,1)}, u32[]{:S(2)}, u32[]{:S(2)}) %all-to-all-start) | async-done | bytes 524320 | tf_op jit(solution)/shard_map/all_to_all | solution.py:253
  99.5 1.4 copy-done.1
  100.9 1.4 copy-done.4
  102.3 2.2 shard_map.130
  105.4 18.2 %all_to_all.20.parts_ref = bf16[4,32,3072]{2,1,0:T(8,128)(2,1)S(1)} all-to-all(bf16[4,32,3072]{2,1,0:T(8,128)(2,1)S(1)} %bitcast.19), channel_id=1, replica_groups=mesh['yh'=2,'yl'=2,'xh'=2,'core'=2,'replica'=64] {'xh','yh'}, dimensions={0} | all-to-all | bytes 1572864 | tf_op jit(solution)/shard_map/all_to_all | solution.py:253
  123.8 14.2 %all_to_all.21 = bf16[4,32,3072]{2,1,0:T(8,128)(2,1)S(1)} all-to-all(bf16[4,32,3072]{2,1,0:T(8,128)(2,1)S(1)} %shard_map.131), channel_id=1, replica_groups=mesh['yh'=2,'yl'=2,'xh'=2,'core'=2,'replica'=64] {'xh','yh'}, dimensions={0} | all-to-all | bytes 1572864 | tf_op jit(solution)/shard_map/all_to_all | solution.py:253
  138.0 2.5 %shard_map.132 = bf16[2048,128]{1,0:T(8,128)(2,1)S(1)} custom-call(bf16[128,3072]{1,0:T(8,128)(2,1)S(1)} %bitcast.16, bf16[768,1024]{1,0:T(8,128)(2,1)S(1)} %shard_map.129.w0, bf16[768,1024]{1,0:T(8,128)(2,1)S(1)} %copy-done.2, bf16[768,1024]{1,0:T(8,128)(2,1)S(1)} %collective-permute-done.1.w2, bf16[768,1024]{1,0:T(8,128)(2,1)S(1)} %copy-done.5), custom_call_target="tpu_custom_call" | custom-call | flops 805306368 | bytes 6291456 | tf_op jit(solution)/shard_map/pallas_call | solution.py:304
  141.4 23.5 %all-to-all-start.3 = ((bf16[256,8,128]{2,1,0:T(8,128)(2,1)}), bf16[256,8,128]{2,1,0:T(8,128)(2,1)}, u32[]{:S(2)}, u32[]{:S(2)}) async-start(bf16[256,8,128]{2,1,0:T(8,128)(2,1)} %bitcast.18), calls=%async_computation.3 | async-start | bytes 1048576 | tf_op jit(solution)/shard_map/all_to_all | solution.py:253
  167.1 1.8 shard_map.134
  168.9 3.4 %collective-permute-start.3 = (bf16[2,768,1024]{2,1,0:T(8,128)(2,1)S(1)}, bf16[2,768,1024]{2,1,0:T(8,128)(2,1)S(1)}, u32[]{:S(2)}, u32[]{:S(2)}) collective-permute-start(bf16[2,768,1024]{2,1,0:T(8,128)(2,1)S(1)} %get-tuple-element.25), channel_id=1, source_target_pairs={{0,64},{64,0},{1,65},{65,1},{2,66},{66,2},{3,67},{67,3},{4,68},{68... | collective-permute-start | bytes 9437192 | tf_op jit(solution)/shard_map/ppermute | solution.py:319
  172.4 5.3 %collective-permute-done.3.came_ref = bf16[2,768,1024]{2,1,0:T(8,128)(2,1)S(1)} collective-permute-done((bf16[2,768,1024]{2,1,0:T(8,128)(2,1)S(1)}, bf16[2,768,1024]{2,1,0:T(8,128)(2,1)S(1)}, u32[]{:S(2)}, u32[]{:S(2)}) %collective-permute-start.3) | collective-permute-done | bytes 3145760 | tf_op jit(solution)/shard_map/ppermute | solution.py:319
  177.6 1.8 shard_map.135
  179.5 3.0 %collective-permute-start.4 = (bf16[768,1024]{1,0:T(8,128)(2,1)}, bf16[768,1024]{1,0:T(8,128)(2,1)S(1)}, u32[]{:S(2)}, u32[]{:S(2)}) collective-permute-start(bf16[768,1024]{1,0:T(8,128)(2,1)} %get-tuple-element.27), channel_id=1, source_target_pairs={{0,256},{256,0},{1,257},{257,1},{2,258},{258,2},{3,259},{259,3},{4... | collective-permute-start | bytes 4718600 | tf_op jit(solution)/shard_map/ppermute | solution.py:321
  182.4 43.1 %all-to-all-done.3 = bf16[256,8,128]{2,1,0:T(8,128)(2,1)} async-done(((bf16[256,8,128]{2,1,0:T(8,128)(2,1)}), bf16[256,8,128]{2,1,0:T(8,128)(2,1)}, u32[]{:S(2)}, u32[]{:S(2)}) %all-to-all-start.3) | async-done | bytes 524320 | tf_op jit(solution)/shard_map/all_to_all | solution.py:253
  225.6 2.0 shard_map.133
  227.6 1.5 shard_map.136
  (31 shorter events, 8.4 us)
Async XLA Ops:
  2.9 96.6 %all-to-all-start = ((bf16[256,8,128]{2,1,0:T(8,128)(2,1)}), bf16[256,8,128]{2,1,0:T(8,128)(2,1)}, u32[]{:S(2)}, u32[]{:S(2)}) async-start(bf16[256,8,128]{2,1,0:T(8,128)(2,1)} %bitcast.23), calls=%async_computation | async-start | bytes 1048576 | tf_op jit(solution)/shard_map/all_to_all | solution.py:253
  38.9 1.0 copy-start.9
  39.9 1.0 copy-start.10
  41.0 1.0 copy-start.11
  42.2 42.4 %collective-permute-start.1 = (bf16[768,1024]{1,0:T(8,128)(2,1)S(1)}, bf16[768,1024]{1,0:T(8,128)(2,1)S(1)}, u32[]{:S(2)}, u32[]{:S(2)}) collective-permute-start(bf16[768,1024]{1,0:T(8,128)(2,1)S(1)} %shard_map.129.w0), channel_id=1, source_target_pairs={{0,256},{256,0},{1,257},{257,1},{2,258},{258,2},{3,259},{259,3},{4... | collective-permute-start | bytes 4718600 | tf_op jit(solution)/shard_map/ppermute | solution.py:282
  46.4 41.7 %collective-permute-start = (bf16[768,1024]{1,0:T(8,128)(2,1)S(1)}, bf16[768,1024]{1,0:T(8,128)(2,1)S(1)}, u32[]{:S(2)}, u32[]{:S(2)}) collective-permute-start(bf16[768,1024]{1,0:T(8,128)(2,1)S(1)} %shard_map.129.w0), channel_id=1, source_target_pairs={{0,64},{64,0},{1,65},{65,1},{2,66},{66,2},{3,67},{67,3},{4,68},{68... | collective-permute-start | bytes 4718600 | tf_op jit(solution)/shard_map/ppermute | solution.py:283
  84.6 6.4 %collective-permute-start.2 = (bf16[768,1024]{1,0:T(8,128)(2,1)S(1)}, bf16[768,1024]{1,0:T(8,128)(2,1)S(1)}, u32[]{:S(2)}, u32[]{:S(2)}) collective-permute-start(bf16[768,1024]{1,0:T(8,128)(2,1)S(1)} %collective-permute-done.1.w2), channel_id=1, source_target_pairs={{0,64},{64,0},{1,65},{65,1},{2,66},{66,2},{3,67},{67,3},{4,68},{68... | collective-permute-start | bytes 4718600 | tf_op jit(solution)/shard_map/ppermute | solution.py:284
  88.1 1.2 copy-start
  91.1 1.1 copy-start.3
  99.5 1.4 copy-start.1
  100.9 1.4 copy-start.4
  104.6 0.8 copy-start.12
  123.6 14.4 %copy-start.2 = (bf16[768,1024]{1,0:T(8,128)(2,1)S(1)}, bf16[768,1024]{1,0:T(8,128)(2,1)}, u32[]{:S(2)}) copy-start(bf16[768,1024]{1,0:T(8,128)(2,1)} %copy-done) | copy-start | bytes 4718596
  123.6 14.4 %copy-start.5 = (bf16[768,1024]{1,0:T(8,128)(2,1)S(1)}, bf16[768,1024]{1,0:T(8,128)(2,1)}, u32[]{:S(2)}) copy-start(bf16[768,1024]{1,0:T(8,128)(2,1)} %copy-done.3) | copy-start | bytes 4718596
  138.0 2.6 %copy-start.6 = (bf16[4,32,3072]{2,1,0:T(8,128)(2,1)}, bf16[4,32,3072]{2,1,0:T(8,128)(2,1)S(1)}, u32[]{:S(2)}) copy-start(bf16[4,32,3072]{2,1,0:T(8,128)(2,1)S(1)} %all_to_all.21) | copy-start | bytes 2359300
  140.6 0.8 copy-start.8
  141.4 84.2 %all-to-all-start.3 = ((bf16[256,8,128]{2,1,0:T(8,128)(2,1)}), bf16[256,8,128]{2,1,0:T(8,128)(2,1)}, u32[]{:S(2)}, u32[]{:S(2)}) async-start(bf16[256,8,128]{2,1,0:T(8,128)(2,1)} %bitcast.18), calls=%async_computation.3 | async-start | bytes 1048576 | tf_op jit(solution)/shard_map/all_to_all | solution.py:253
  164.9 1.1 copy-start.7
  166.1 1.0 copy-start.13
  168.9 8.7 %collective-permute-start.3 = (bf16[2,768,1024]{2,1,0:T(8,128)(2,1)S(1)}, bf16[2,768,1024]{2,1,0:T(8,128)(2,1)S(1)}, u32[]{:S(2)}, u32[]{:S(2)}) collective-permute-start(bf16[2,768,1024]{2,1,0:T(8,128)(2,1)S(1)} %get-tuple-element.25), channel_id=1, source_target_pairs={{0,64},{64,0},{1,65},{65,1},{2,66},{66,2},{3,67},{67,3},{4,68},{68... | collective-permute-start | bytes 9437192 | tf_op jit(solution)/shard_map/ppermute | solution.py:319
  177.6 47.9 %copy-start.14 = (bf16[2,128,256]{2,1,0:T(8,128)(2,1)S(1)}, bf16[2,128,256]{2,1,0:T(8,128)(2,1)}, u32[]{:S(2)}) copy-start(bf16[2,128,256]{2,1,0:T(8,128)(2,1)} %get-tuple-element.18.table_ref) | copy-start | bytes 393220
  179.5 48.1 %collective-permute-start.4 = (bf16[768,1024]{1,0:T(8,128)(2,1)}, bf16[768,1024]{1,0:T(8,128)(2,1)S(1)}, u32[]{:S(2)}, u32[]{:S(2)}) collective-permute-start(bf16[768,1024]{1,0:T(8,128)(2,1)} %get-tuple-element.27), channel_id=1, source_target_pairs={{0,256},{256,0},{1,257},{257,1},{2,258},{258,2},{3,259},{259,3},{4... | collective-permute-start | bytes 4718600 | tf_op jit(solution)/shard_map/ppermute | solution.py:321

commit v4 on v3

--- a/solution.py
+++ b/solution.py
@@ -20,6 +20,8 @@
 SLOTS = 2
 TILE = 8
 LANE = 128
+ROOM = 50
+LARGE = 60
 
 
 def mm(a, b, dims):
@@ -106,11 +108,19 @@
     out_ref[2 * width : 3 * width, :] = down_ref[...].T
 
 
-def partial_kernel(came_ref, w0, w1, w2, w3, x_ref, out_ref, rows_ref, stage_ref):
+def partial_kernel(came_ref, w0, w1, w2, w3, x_ref, out_ref, rows_ref, stage_ref, held, sem):
     peers = came_ref.shape[0] // TILE
     blocks = peers // QUAD
     hidden = w0.shape[1]
     width = w0.shape[0] // 3
+    fetches = []
+    for part in range(3):
+        for k, w in enumerate((w0, w1, w2, w3)):
+            at = pl.ds(part * width, width)
+            fetches.append(
+                pltpu.make_async_copy(w.at[at, :], held.at[k, at, :], sem.at[QUAD * part + k])
+            )
+            fetches[-1].start()
     wide = QUAD * width
     rows_ref[...] = came_ref[...].astype(f32)
     for j in range(TILE):
@@ -126,10 +136,13 @@
                 ]
     for part in range(3):
         total = jnp.zeros((SLOTS * blocks, hidden), f32)
-        for k, w in enumerate((w0, w1, w2, w3)):
+        for k in range(QUAD):
             column = (part // 2) * wide + k * width
+            fetches[QUAD * part + k].wait()
             total = total + mm(
-                x_ref[:, column : column + width], w[part * width : (part + 1) * width, :], NN
+                x_ref[:, column : column + width],
+                held[k, part * width : (part + 1) * width, :],
+                NN,
             )
         out_ref[:, part * hidden : (part + 1) * hidden] = total.astype(bf16)
 
@@ -155,7 +168,11 @@
         out_ref[g, :, 2 * hidden : 3 * hidden] = up_cot
 
 
-def back_kernel(hgu_ref, w0, w1, w2, w3, send_ref, stage_ref, rows_ref):
+def back_kernel(hgu_ref, w0, w1, w2, w3, send_ref, stage_ref, rows_ref, held, sem):
+    fetches = []
+    for k, w in enumerate((w0, w1, w2, w3)):
+        fetches.append(pltpu.make_async_copy(w, held.at[k], sem.at[k]))
+        fetches[-1].start()
     hidden = w0.shape[1]
     width = w0.shape[0] // 3
     blocks = hgu_ref.shape[0] // SLOTS
@@ -164,9 +181,12 @@
     inner = hgu_ref[:, 0:hidden]
     gate_cot = hgu_ref[:, hidden : 2 * hidden]
     up_cot = hgu_ref[:, 2 * hidden : 3 * hidden]
-    for k, w in enumerate((w0, w1, w2, w3)):
-        out = mm(inner, w[2 * width : 3 * width, :], NT)
-        back = mm(gate_cot, w[0:width, :], NT) + mm(up_cot, w[width : 2 * width, :], NT)
+    for k in range(QUAD):
+        fetches[k].wait()
+        out = mm(inner, held[k, 2 * width : 3 * width, :], NT)
+        back = mm(gate_cot, held[k, 0:width, :], NT) + mm(
+            up_cot, held[k, width : 2 * width, :], NT
+        )
         at = pl.ds(pl.multiple_of((mine ^ k) * blocks, blocks), blocks)
         for s in range(SLOTS):
             rows = slice(s * blocks, (s + 1) * blocks)
@@ -276,7 +296,7 @@
     )(*arrays)
     came = messages(send)
 
-    w0 = call(gather_kernel, shape((3 * width, hidden), bf16), 0, 12 * width * hidden)(
+    w0 = call(gather_kernel, shape((3 * width, hidden), bf16), 0, 12 * width * hidden, ROOM)(
         gate_weight[0], up_weight[0], down_weight[0]
     )
     w2 = lax.ppermute(w0, "yl", flip)
@@ -288,9 +308,14 @@
         (shape((rows, 2 * QUAD * width), bf16), shape((rows, 3 * hidden), bf16)),
         3 * product,
         weight_bytes,
+        ROOM,
+        in_specs=[pl.BlockSpec(memory_space=pltpu.VMEM)]
+        + [pl.BlockSpec(memory_space=pl.ANY)] * QUAD,
         scratch_shapes=[
             pltpu.VMEM((peers * TILE, LANE), f32),
             pltpu.VMEM((TILE, peers, LANE), bf16),
+            pltpu.VMEM((QUAD, 3 * width, hidden), bf16),
+            pltpu.SemaphoreType.DMA((3 * QUAD,)),
         ],
     )(came, w0, w1, w2, w3)
     parts = spread(partial.reshape(groups, rows // groups, 3 * hidden), others)
@@ -306,18 +331,25 @@
         message,
         3 * product,
         weight_bytes,
+        ROOM,
+        in_specs=[pl.BlockSpec(memory_space=pltpu.VMEM)]
+        + [pl.BlockSpec(memory_space=pl.ANY)] * QUAD,
         scratch_shapes=[
             pltpu.VMEM((TILE, peers, LANE), f32),
             pltpu.VMEM((peers * TILE, LANE), f32),
+            pltpu.VMEM((QUAD, 3 * width, hidden), bf16),
+            pltpu.SemaphoreType.DMA((QUAD,)),
         ],
     )(hgu, w0, w1, w2, w3)
 
     pair = shape((2, 3 * width, hidden), bf16)
     one = shape((3 * width, hidden), bf16)
     returned = messages(sent_back)
-    keep, give = call(grads_kernel, (pair, pair), 3 * product, weight_bytes)(x, hgu)
+    keep, give = call(grads_kernel, (pair, pair), 3 * product, weight_bytes, LARGE)(x, hgu)
     got = lax.ppermute(give, "core", flip)
-    own, other = call(first_sum_kernel, (one, one), 6 * width * hidden, 2 * weight_bytes)(keep, got)
+    own, other = call(
+        first_sum_kernel, (one, one), 6 * width * hidden, 2 * weight_bytes, LARGE
+    )(keep, got)
     theirs = lax.ppermute(other, "yl", flip)
     grads = call(
         last_sum_kernel,

time: 230 us -> 227 us (0.987)
  Pallas kernels: 14.6 us -> 24.2 us
  local copies, waits for them, and re-layouts: 12 us -> 6.44 us
  starting transfers between devices: 75.6 us -> 71.8 us
  waiting for transfers between devices: 93.6 us -> 90.4 us
    pallas_call x3, Pallas kernels: 6.18 us -> 16.1 us  [the longest x1 5.83 us: local(): call(back_kernel, message, 3 * product, weight_bytes, ROOM, in_specs=[pl....]
    unnamed x30 -> x20, local copies, waits for them, and re-layouts: 12 us -> 6.44 us
    all_to_all x2, starting transfers between devices: 59.5 us -> 55.7 us  [spread(): return lax.all_to_all(x, axis, split_axis=0, concat_axis=0, tiled=True)]
    all_to_all x2, waiting for transfers between devices: 50.4 us -> 46.7 us  [spread(): return lax.all_to_all(x, axis, split_axis=0, concat_axis=0, tiled=True)]
  transfers between devices with their start and end apart: 7 -> 7, of which waited for: 5 -> 5; matrix products, arithmetic and copies ran while one was open for 0% -> 0% of each run, Pallas kernels for 3% -> 5%
where the time goes in v4:
time: 227 us; the launch traced here: 226 us
  waiting for transfers between devices  90.4 us (40%)
  starting transfers between devices  71.8 us (32%)
  blocking collectives  32.3 us (14%)
  Pallas kernels  24.2 us (11%)
  local copies, waits for them, and re-layouts  6.44 us (3%)
    all_to_all x2, starting transfers between devices, spread(): return lax.all_to_all(x, axis, split_axis=0, concat_axis=0, tiled=True)  55.7 us
    all_to_all x2, waiting for transfers between devices, spread(): return lax.all_to_all(x, axis, split_axis=0, concat_axis=0, tiled=True)  46.7 us
    ppermute x1, waiting for transfers between devices, local(): w2 = lax.ppermute(w0, 'yl', flip)  36.2 us
    all_to_all x2, blocking collectives, spread(): return lax.all_to_all(x, axis, split_axis=0, concat_axis=0, tiled=True)  32.3 us
    unnamed x20, local copies, waits for them, and re-layouts  6.44 us
    pallas_call x1, Pallas kernels, local(): call(back_kernel, message, 3 * product, weight_bytes, ROOM, in_specs=[pl....  5.83 us
    ppermute x1, waiting for transfers between devices, local(): got = lax.ppermute(give, 'core', flip)  5.47 us
    pallas_call x1, Pallas kernels, local(): call(grads_kernel, (pair, pair), 3 * product, weight_bytes, LARGE)(x, hgu)  5.37 us
  transfers between devices with their start and end apart: 7, of which 5 were waited for; matrix products, arithmetic and copies ran while one was open for 0% of the time, Pallas kernels for 5%

profile of v4, /device:TPU:1, one launch (start us, length us, event | category | flops | bytes accessed | tf_op | source)
XLA Modules:
  0.0 226.0 jit_solution(12673134289363200284)
XLA Ops:
  0.6 2.3 %shard_map.128 = (bf16[2048,128]{1,0:T(8,128)(2,1)}, bf16[2,128,256]{2,1,0:T(8,128)(2,1)}) custom-call(bf16[32,256]{1,0:T(8,128)(2,1)} %refs_0_.1, bf16[32,256]{1,0:T(8,128)(2,1)} %refs_1_.1, f32[8,32]{1,0:T(8,128)} %bitcast.28, s32[8,32]{1,0:T(8,128)} %bitcast.29, s32[1,32]{1,0:T(1,128)} %bitcast.31, f32[1,256]{1,0:T(1,128)} %bitcast.30), custom_call_target="tpu_custom_call" | custom-call | flops 33554432 | bytes 1048576 | tf_op jit(solution)/shard_map/pallas_call | solution.py:286
  2.9 35.0 %all-to-all-start = ((bf16[256,8,128]{2,1,0:T(8,128)(2,1)}), bf16[256,8,128]{2,1,0:T(8,128)(2,1)S(1)}, u32[]{:S(2)}, u32[]{:S(2)}) async-start(bf16[256,8,128]{2,1,0:T(8,128)(2,1)} %bitcast.24), calls=%async_computation | async-start | bytes 1048576 | tf_op jit(solution)/shard_map/all_to_all | solution.py:273
  38.9 1.0 copy-done.3
  40.0 1.0 copy-done.4
  41.2 4.1 %collective-permute-start.1 = (bf16[768,1024]{1,0:T(8,128)(2,1)S(1)}, bf16[768,1024]{1,0:T(8,128)(2,1)S(1)}, u32[]{:S(2)}, u32[]{:S(2)}) collective-permute-start(bf16[768,1024]{1,0:T(8,128)(2,1)S(1)} %shard_map.129.w0), channel_id=1, source_target_pairs={{0,256},{256,0},{1,257},{257,1},{2,258},{258,2},{3,259},{259,3},{4... | collective-permute-start | bytes 4718600 | tf_op jit(solution)/shard_map/ppermute | solution.py:302
  45.4 2.1 collective-permute-start
  47.5 36.2 %collective-permute-done.1.w2 = bf16[768,1024]{1,0:T(8,128)(2,1)S(1)} collective-permute-done((bf16[768,1024]{1,0:T(8,128)(2,1)S(1)}, bf16[768,1024]{1,0:T(8,128)(2,1)S(1)}, u32[]{:S(2)}, u32[]{:S(2)}) %collective-permute-start.1) | collective-permute-done | bytes 1572896 | tf_op jit(solution)/shard_map/ppermute | solution.py:302
  83.7 3.4 %collective-permute-start.2 = (bf16[768,1024]{1,0:T(8,128)(2,1)S(1)}, bf16[768,1024]{1,0:T(8,128)(2,1)}, u32[]{:S(2)}, u32[]{:S(2)}) collective-permute-start(bf16[768,1024]{1,0:T(8,128)(2,1)S(1)} %collective-permute-done.1.w2), channel_id=1, source_target_pairs={{0,64},{64,0},{1,65},{65,1},{2,66},{66,2},{3,67},{67,3},{4,68},{68... | collective-permute-start | bytes 4718600 | tf_op jit(solution)/shard_map/ppermute | solution.py:304
  87.2 1.1 copy-done.8
  88.3 2.0 collective-permute-done.2.w3
  90.3 9.1 %all-to-all-done = bf16[256,8,128]{2,1,0:T(8,128)(2,1)S(1)} async-done(((bf16[256,8,128]{2,1,0:T(8,128)(2,1)}), bf16[256,8,128]{2,1,0:T(8,128)(2,1)S(1)}, u32[]{:S(2)}, u32[]{:S(2)}) %all-to-all-start) | async-done | bytes 524320 | tf_op jit(solution)/shard_map/all_to_all | solution.py:273
  99.4 2.9 %shard_map.130 = (bf16[128,2048]{1,0:T(8,128)(2,1)S(1)}, bf16[128,3072]{1,0:T(8,128)(2,1)S(1)}) custom-call(bf16[2048,128]{1,0:T(8,128)(2,1)S(1)} %bitcast.18, bf16[768,1024]{1,0:T(8,128)(2,1)S(1)} %shard_map.129.w0, bf16[768,1024]{1,0:T(8,128)(2,1)} %copy-done.8, bf16[768,1024]{1,0:T(8,128)(2,1)} %copy-done.7, bf16[768,1024]{1,0:T(8,128)(2,1)} %collective-permute-done.2.w3), custom_call_target="tpu_custom_call" | custom-call | flops 805306368 | bytes 6291456 | tf_op jit(solution)/shard_map/pallas_call | solution.py:306
  102.4 18.2 %all_to_all.20.parts_ref = bf16[4,32,3072]{2,1,0:T(8,128)(2,1)S(1)} all-to-all(bf16[4,32,3072]{2,1,0:T(8,128)(2,1)S(1)} %bitcast.19), channel_id=1, replica_groups=mesh['yh'=2,'yl'=2,'xh'=2,'core'=2,'replica'=64] {'xh','yh'}, dimensions={0} | all-to-all | bytes 1572864 | tf_op jit(solution)/shard_map/all_to_all | solution.py:273
  120.8 14.1 %all_to_all.21 = bf16[4,32,3072]{2,1,0:T(8,128)(2,1)S(1)} all-to-all(bf16[4,32,3072]{2,1,0:T(8,128)(2,1)S(1)} %shard_map.131), channel_id=1, replica_groups=mesh['yh'=2,'yl'=2,'xh'=2,'core'=2,'replica'=64] {'xh','yh'}, dimensions={0} | all-to-all | bytes 1572864 | tf_op jit(solution)/shard_map/all_to_all | solution.py:273
  134.9 5.8 %shard_map.132 = bf16[2048,128]{1,0:T(8,128)(2,1)} custom-call(bf16[128,3072]{1,0:T(8,128)(2,1)S(1)} %bitcast.16, bf16[768,1024]{1,0:T(8,128)(2,1)S(1)} %shard_map.129.w0, bf16[768,1024]{1,0:T(8,128)(2,1)} %copy-done.8, bf16[768,1024]{1,0:T(8,128)(2,1)} %copy-done.7, bf16[768,1024]{1,0:T(8,128)(2,1)} %collective-permute-done.2.w3), custom_call_target="tpu_custom_call" | custom-call | flops 805306368 | bytes 6291456 | tf_op jit(solution)/shard_map/pallas_call | solution.py:329
  140.7 20.8 %all-to-all-start.3 = ((bf16[256,8,128]{2,1,0:T(8,128)(2,1)}), bf16[256,8,128]{2,1,0:T(8,128)(2,1)S(1)}, u32[]{:S(2)}, u32[]{:S(2)}) async-start(bf16[256,8,128]{2,1,0:T(8,128)(2,1)} %bitcast.11), calls=%async_computation.3 | async-start | bytes 1048576 | tf_op jit(solution)/shard_map/all_to_all | solution.py:273
  161.5 5.4 %shard_map.134 = (bf16[2,768,1024]{2,1,0:T(8,128)(2,1)}, bf16[2,768,1024]{2,1,0:T(8,128)(2,1)}) custom-call(bf16[128,2048]{1,0:T(8,128)(2,1)} %copy-done.5, bf16[128,3072]{1,0:T(8,128)(2,1)} %bitcast.17), custom_call_target="tpu_custom_call" | custom-call | flops 805306368 | bytes 6291456 | tf_op jit(solution)/shard_map/pallas_call | solution.py:348
  166.9 3.3 %collective-permute-start.3 = (bf16[2,768,1024]{2,1,0:T(8,128)(2,1)}, bf16[2,768,1024]{2,1,0:T(8,128)(2,1)S(1)}, u32[]{:S(2)}, u32[]{:S(2)}) collective-permute-start(bf16[2,768,1024]{2,1,0:T(8,128)(2,1)} %get-tuple-element.25), channel_id=1, source_target_pairs={{0,64},{64,0},{1,65},{65,1},{2,66},{66,2},{3,67},{67,3},{4,68},{68... | collective-permute-start | bytes 9437192 | tf_op jit(solution)/shard_map/ppermute | solution.py:349
  170.2 5.5 %collective-permute-done.3.came_ref = bf16[2,768,1024]{2,1,0:T(8,128)(2,1)S(1)} collective-permute-done((bf16[2,768,1024]{2,1,0:T(8,128)(2,1)}, bf16[2,768,1024]{2,1,0:T(8,128)(2,1)S(1)}, u32[]{:S(2)}, u32[]{:S(2)}) %collective-permute-start.3) | collective-permute-done | bytes 3145760 | tf_op jit(solution)/shard_map/ppermute | solution.py:349
  175.7 1.7 copy-done.9
  177.4 4.9 %shard_map.135 = (bf16[768,1024]{1,0:T(8,128)(2,1)}, bf16[768,1024]{1,0:T(8,128)(2,1)}) custom-call(bf16[2,768,1024]{2,1,0:T(8,128)(2,1)} %get-tuple-element.24.keep_ref, bf16[2,768,1024]{2,1,0:T(8,128)(2,1)} %copy-done.9), custom_call_target="tpu_custom_call" | custom-call | flops 1572864 | bytes 12582912 | tf_op jit(solution)/shard_map/pallas_call | solution.py:350
  182.3 3.0 %collective-permute-start.4 = (bf16[768,1024]{1,0:T(8,128)(2,1)}, bf16[768,1024]{1,0:T(8,128)(2,1)S(1)}, u32[]{:S(2)}, u32[]{:S(2)}) collective-permute-start(bf16[768,1024]{1,0:T(8,128)(2,1)} %get-tuple-element.27), channel_id=1, source_target_pairs={{0,256},{256,0},{1,257},{257,1},{2,258},{258,2},{3,259},{259,3},{4... | collective-permute-start | bytes 4718600 | tf_op jit(solution)/shard_map/ppermute | solution.py:353
  185.4 37.6 %all-to-all-done.3 = bf16[256,8,128]{2,1,0:T(8,128)(2,1)S(1)} async-done(((bf16[256,8,128]{2,1,0:T(8,128)(2,1)}), bf16[256,8,128]{2,1,0:T(8,128)(2,1)S(1)}, u32[]{:S(2)}, u32[]{:S(2)}) %all-to-all-start.3) | async-done | bytes 524320 | tf_op jit(solution)/shard_map/all_to_all | solution.py:273
  224.5 1.5 shard_map.136
  (21 shorter events, 2.9 us)
Async XLA Ops:
  2.9 96.5 %all-to-all-start = ((bf16[256,8,128]{2,1,0:T(8,128)(2,1)}), bf16[256,8,128]{2,1,0:T(8,128)(2,1)S(1)}, u32[]{:S(2)}, u32[]{:S(2)}) async-start(bf16[256,8,128]{2,1,0:T(8,128)(2,1)} %bitcast.24), calls=%async_computation | async-start | bytes 1048576 | tf_op jit(solution)/shard_map/all_to_all | solution.py:273
  37.9 1.0 copy-start.2
  38.9 1.0 copy-start.3
  40.0 1.0 copy-start.4
  41.2 42.5 %collective-permute-start.1 = (bf16[768,1024]{1,0:T(8,128)(2,1)S(1)}, bf16[768,1024]{1,0:T(8,128)(2,1)S(1)}, u32[]{:S(2)}, u32[]{:S(2)}) collective-permute-start(bf16[768,1024]{1,0:T(8,128)(2,1)S(1)} %shard_map.129.w0), channel_id=1, source_target_pairs={{0,256},{256,0},{1,257},{257,1},{2,258},{258,2},{3,259},{259,3},{4... | collective-permute-start | bytes 4718600 | tf_op jit(solution)/shard_map/ppermute | solution.py:302
  45.4 41.8 %collective-permute-start = (bf16[768,1024]{1,0:T(8,128)(2,1)S(1)}, bf16[768,1024]{1,0:T(8,128)(2,1)S(1)}, u32[]{:S(2)}, u32[]{:S(2)}) collective-permute-start(bf16[768,1024]{1,0:T(8,128)(2,1)S(1)} %shard_map.129.w0), channel_id=1, source_target_pairs={{0,64},{64,0},{1,65},{65,1},{2,66},{66,2},{3,67},{67,3},{4,68},{68... | collective-permute-start | bytes 4718600 | tf_op jit(solution)/shard_map/ppermute | solution.py:303
  83.7 3.4 %copy-start.7 = (bf16[768,1024]{1,0:T(8,128)(2,1)}, bf16[768,1024]{1,0:T(8,128)(2,1)S(1)}, u32[]{:S(2)}) copy-start(bf16[768,1024]{1,0:T(8,128)(2,1)S(1)} %collective-permute-done.1.w2) | copy-start | bytes 4718596
  83.7 6.6 %collective-permute-start.2 = (bf16[768,1024]{1,0:T(8,128)(2,1)S(1)}, bf16[768,1024]{1,0:T(8,128)(2,1)}, u32[]{:S(2)}, u32[]{:S(2)}) collective-permute-start(bf16[768,1024]{1,0:T(8,128)(2,1)S(1)} %collective-permute-done.1.w2), channel_id=1, source_target_pairs={{0,64},{64,0},{1,65},{65,1},{2,66},{66,2},{3,67},{67,3},{4,68},{68... | collective-permute-start | bytes 4718600 | tf_op jit(solution)/shard_map/ppermute | solution.py:304
  87.2 1.2 copy-start.8
  102.4 18.4 %copy-start.5 = (bf16[128,2048]{1,0:T(8,128)(2,1)}, bf16[128,2048]{1,0:T(8,128)(2,1)S(1)}, u32[]{:S(2)}) copy-start(bf16[128,2048]{1,0:T(8,128)(2,1)S(1)} %get-tuple-element.23.x_ref) | copy-start | bytes 1572868
  134.9 5.8 %copy-start = (bf16[4,32,3072]{2,1,0:T(8,128)(2,1)}, bf16[4,32,3072]{2,1,0:T(8,128)(2,1)S(1)}, u32[]{:S(2)}) copy-start(bf16[4,32,3072]{2,1,0:T(8,128)(2,1)S(1)} %all_to_all.21) | copy-start | bytes 2359300
  140.7 82.3 %all-to-all-start.3 = ((bf16[256,8,128]{2,1,0:T(8,128)(2,1)}), bf16[256,8,128]{2,1,0:T(8,128)(2,1)S(1)}, u32[]{:S(2)}, u32[]{:S(2)}) async-start(bf16[256,8,128]{2,1,0:T(8,128)(2,1)} %bitcast.11), calls=%async_computation.3 | async-start | bytes 1048576 | tf_op jit(solution)/shard_map/all_to_all | solution.py:273
  166.9 8.8 %collective-permute-start.3 = (bf16[2,768,1024]{2,1,0:T(8,128)(2,1)}, bf16[2,768,1024]{2,1,0:T(8,128)(2,1)S(1)}, u32[]{:S(2)}, u32[]{:S(2)}) collective-permute-start(bf16[2,768,1024]{2,1,0:T(8,128)(2,1)} %get-tuple-element.25), channel_id=1, source_target_pairs={{0,64},{64,0},{1,65},{65,1},{2,66},{66,2},{3,67},{67,3},{4,68},{68... | collective-permute-start | bytes 9437192 | tf_op jit(solution)/shard_map/ppermute | solution.py:349
  175.7 1.7 copy-start.9
  177.4 45.6 %copy-start.6 = (bf16[2,128,256]{2,1,0:T(8,128)(2,1)S(1)}, bf16[2,128,256]{2,1,0:T(8,128)(2,1)}, u32[]{:S(2)}) copy-start(bf16[2,128,256]{2,1,0:T(8,128)(2,1)} %get-tuple-element.18.table_ref) | copy-start | bytes 393220
  182.3 41.7 %collective-permute-start.4 = (bf16[768,1024]{1,0:T(8,128)(2,1)}, bf16[768,1024]{1,0:T(8,128)(2,1)S(1)}, u32[]{:S(2)}, u32[]{:S(2)}) collective-permute-start(bf16[768,1024]{1,0:T(8,128)(2,1)} %get-tuple-element.27), channel_id=1, source_target_pairs={{0,256},{256,0},{1,257},{257,1},{2,258},{258,2},{3,259},{259,3},{4... | collective-permute-start | bytes 4718600 | tf_op jit(solution)/shard_map/ppermute | solution.py:353
  223.0 1.4 copy-start.1

commit v5 on v4

--- a/solution.py
+++ b/solution.py
@@ -169,12 +169,16 @@
 
 
 def back_kernel(hgu_ref, w0, w1, w2, w3, send_ref, stage_ref, rows_ref, held, sem):
+    hidden = w0.shape[1]
+    width = w0.shape[0] // 3
     fetches = []
     for k, w in enumerate((w0, w1, w2, w3)):
-        fetches.append(pltpu.make_async_copy(w, held.at[k], sem.at[k]))
-        fetches[-1].start()
-    hidden = w0.shape[1]
-    width = w0.shape[0] // 3
+        for part in range(3):
+            at = pl.ds(part * width, width)
+            fetches.append(
+                pltpu.make_async_copy(w.at[at, :], held.at[k, at, :], sem.at[3 * k + part])
+            )
+            fetches[-1].start()
     blocks = hgu_ref.shape[0] // SLOTS
     peers = QUAD * blocks
     mine = me()
@@ -182,7 +186,8 @@
     gate_cot = hgu_ref[:, hidden : 2 * hidden]
     up_cot = hgu_ref[:, 2 * hidden : 3 * hidden]
     for k in range(QUAD):
-        fetches[k].wait()
+        for fetch in fetches[3 * k : 3 * k + 3]:
+            fetch.wait()
         out = mm(inner, held[k, 2 * width : 3 * width, :], NT)
         back = mm(gate_cot, held[k, 0:width, :], NT) + mm(
             up_cot, held[k, width : 2 * width, :], NT
@@ -199,19 +204,29 @@
     send_ref[...] = rows_ref[...].astype(bf16)
 
 
-def grads_kernel(x_ref, hgu_ref, keep_ref, send_ref):
+def grads_kernel(x_ref, hgu_ref, keep_ref, send_ref, made, sem):
     hidden = hgu_ref.shape[1] // 3
     width = keep_ref.shape[1] // 3
     wide = QUAD * width
-    for k in range(QUAD):
+    writes = []
+    for k in (1, 3, 0, 2):
         out_ref = send_ref if k % 2 else keep_ref
         for part, (column, factor) in enumerate(((0, 1), (0, 2), (1, 0))):
             start = column * wide + k * width
-            out_ref[k // 2, part * width : (part + 1) * width, :] = mm(
+            at = pl.ds(part * width, width)
+            made[k, at, :] = mm(
                 x_ref[:, start : start + width],
                 hgu_ref[:, factor * hidden : (factor + 1) * hidden],
                 TN,
             ).astype(bf16)
+            writes.append(
+                pltpu.make_async_copy(
+                    made.at[k, at, :], out_ref.at[k // 2, at, :], sem.at[len(writes)]
+                )
+            )
+            writes[-1].start()
+    for write in writes:
+        write.wait()
 
 
 def first_sum_kernel(keep_ref, came_ref, own_ref, other_ref):
@@ -338,17 +353,35 @@
             pltpu.VMEM((TILE, peers, LANE), f32),
             pltpu.VMEM((peers * TILE, LANE), f32),
             pltpu.VMEM((QUAD, 3 * width, hidden), bf16),
-            pltpu.SemaphoreType.DMA((QUAD,)),
+            pltpu.SemaphoreType.DMA((3 * QUAD,)),
         ],
     )(hgu, w0, w1, w2, w3)
 
     pair = shape((2, 3 * width, hidden), bf16)
     one = shape((3 * width, hidden), bf16)
     returned = messages(sent_back)
-    keep, give = call(grads_kernel, (pair, pair), 3 * product, weight_bytes, LARGE)(x, hgu)
+    keep, give = call(
+        grads_kernel,
+        (pair, pair),
+        3 * product,
+        weight_bytes,
+        LARGE,
+        out_specs=[pl.BlockSpec(memory_space=pl.ANY)] * 2,
+        scratch_shapes=[
+            pltpu.VMEM((QUAD, 3 * width, hidden), bf16),
+            pltpu.SemaphoreType.DMA((3 * QUAD,)),
+        ],
+    )(x, hgu)
     got = lax.ppermute(give, "core", flip)
     own, other = call(
-        first_sum_kernel, (one, one), 6 * width * hidden, 2 * weight_bytes, LARGE
+        first_sum_kernel,
+        (one, one),
+        6 * width * hidden,
+        2 * weight_bytes,
+        LARGE,
+        grid=(6,),
+        in_specs=[pl.BlockSpec((2, width // 2, hidden), lambda i: (0, i, 0))] * 2,
+        out_specs=[pl.BlockSpec((width // 2, hidden), lambda i: (i, 0))] * 2,
     )(keep, got)
     theirs = lax.ppermute(other, "yl", flip)
     grads = call(

time: 227 us -> 227 us (level)
  no operation moved by 1% of the time
where the time goes in v5:
time: 227 us; the launch traced here: 226 us
  waiting for transfers between devices  90.4 us (40%)
  starting transfers between devices  71.8 us (32%)
  blocking collectives  32.3 us (14%)
  Pallas kernels  24.2 us (11%)
  local copies, waits for them, and re-layouts  6.44 us (3%)
    all_to_all x2, starting transfers between devices, spread(): return lax.all_to_all(x, axis, split_axis=0, concat_axis=0, tiled=True)  55.7 us
    all_to_all x2, waiting for transfers between devices, spread(): return lax.all_to_all(x, axis, split_axis=0, concat_axis=0, tiled=True)  46.8 us
    ppermute x1, waiting for transfers between devices, local(): w2 = lax.ppermute(w0, 'yl', flip)  36.2 us
    all_to_all x2, blocking collectives, spread(): return lax.all_to_all(x, axis, split_axis=0, concat_axis=0, tiled=True)  32.3 us
    unnamed x20, local copies, waits for them, and re-layouts  6.44 us
    pallas_call x1, Pallas kernels, local(): call(first_sum_kernel, (one, one), 6 * width * hidden, 2 * weight_bytes,...  5.94 us
    pallas_call x1, Pallas kernels, local(): call(back_kernel, message, 3 * product, weight_bytes, ROOM, in_specs=[pl....  5.86 us
    ppermute x1, waiting for transfers between devices, local(): got = lax.ppermute(give, 'core', flip)  5.47 us
  transfers between devices with their start and end apart: 7, of which 5 were waited for; matrix products, arithmetic and copies ran while one was open for 0% of the time, Pallas kernels for 5%

profile of v5, /device:TPU:1, one launch (start us, length us, event | category | flops | bytes accessed | tf_op | source)
XLA Modules:
  0.0 226.0 jit_solution(17260258411315713089)
XLA Ops:
  0.6 2.3 %shard_map.128 = (bf16[2048,128]{1,0:T(8,128)(2,1)}, bf16[2,128,256]{2,1,0:T(8,128)(2,1)}) custom-call(bf16[32,256]{1,0:T(8,128)(2,1)} %refs_0_.1, bf16[32,256]{1,0:T(8,128)(2,1)} %refs_1_.1, f32[8,32]{1,0:T(8,128)} %bitcast.28, s32[8,32]{1,0:T(8,128)} %bitcast.29, s32[1,32]{1,0:T(1,128)} %bitcast.31, f32[1,256]{1,0:T(1,128)} %bitcast.30), custom_call_target="tpu_custom_call" | custom-call | flops 33554432 | bytes 1048576 | tf_op jit(solution)/shard_map/pallas_call | solution.py:301
  2.9 35.0 %all-to-all-start = ((bf16[256,8,128]{2,1,0:T(8,128)(2,1)}), bf16[256,8,128]{2,1,0:T(8,128)(2,1)S(1)}, u32[]{:S(2)}, u32[]{:S(2)}) async-start(bf16[256,8,128]{2,1,0:T(8,128)(2,1)} %bitcast.24), calls=%async_computation | async-start | bytes 1048576 | tf_op jit(solution)/shard_map/all_to_all | solution.py:288
  38.9 1.0 copy-done.3
  40.0 1.0 copy-done.4
  41.2 4.1 %collective-permute-start.1 = (bf16[768,1024]{1,0:T(8,128)(2,1)S(1)}, bf16[768,1024]{1,0:T(8,128)(2,1)S(1)}, u32[]{:S(2)}, u32[]{:S(2)}) collective-permute-start(bf16[768,1024]{1,0:T(8,128)(2,1)S(1)} %shard_map.129.w0), channel_id=1, source_target_pairs={{0,256},{256,0},{1,257},{257,1},{2,258},{258,2},{3,259},{259,3},{4... | collective-permute-start | bytes 4718600 | tf_op jit(solution)/shard_map/ppermute | solution.py:317
  45.4 2.1 collective-permute-start
  47.5 36.2 %collective-permute-done.1.w2 = bf16[768,1024]{1,0:T(8,128)(2,1)S(1)} collective-permute-done((bf16[768,1024]{1,0:T(8,128)(2,1)S(1)}, bf16[768,1024]{1,0:T(8,128)(2,1)S(1)}, u32[]{:S(2)}, u32[]{:S(2)}) %collective-permute-start.1) | collective-permute-done | bytes 1572896 | tf_op jit(solution)/shard_map/ppermute | solution.py:317
  83.7 3.4 %collective-permute-start.2 = (bf16[768,1024]{1,0:T(8,128)(2,1)S(1)}, bf16[768,1024]{1,0:T(8,128)(2,1)}, u32[]{:S(2)}, u32[]{:S(2)}) collective-permute-start(bf16[768,1024]{1,0:T(8,128)(2,1)S(1)} %collective-permute-done.1.w2), channel_id=1, source_target_pairs={{0,64},{64,0},{1,65},{65,1},{2,66},{66,2},{3,67},{67,3},{4,68},{68... | collective-permute-start | bytes 4718600 | tf_op jit(solution)/shard_map/ppermute | solution.py:319
  87.2 1.1 copy-done.8
  88.3 2.0 collective-permute-done.2.w3
  90.3 9.1 %all-to-all-done = bf16[256,8,128]{2,1,0:T(8,128)(2,1)S(1)} async-done(((bf16[256,8,128]{2,1,0:T(8,128)(2,1)}), bf16[256,8,128]{2,1,0:T(8,128)(2,1)S(1)}, u32[]{:S(2)}, u32[]{:S(2)}) %all-to-all-start) | async-done | bytes 524320 | tf_op jit(solution)/shard_map/all_to_all | solution.py:288
  99.4 2.9 %shard_map.130 = (bf16[128,2048]{1,0:T(8,128)(2,1)S(1)}, bf16[128,3072]{1,0:T(8,128)(2,1)S(1)}) custom-call(bf16[2048,128]{1,0:T(8,128)(2,1)S(1)} %bitcast.18, bf16[768,1024]{1,0:T(8,128)(2,1)S(1)} %shard_map.129.w0, bf16[768,1024]{1,0:T(8,128)(2,1)} %copy-done.8, bf16[768,1024]{1,0:T(8,128)(2,1)} %copy-done.7, bf16[768,1024]{1,0:T(8,128)(2,1)} %collective-permute-done.2.w3), custom_call_target="tpu_custom_call" | custom-call | flops 805306368 | bytes 6291456 | tf_op jit(solution)/shard_map/pallas_call | solution.py:321
  102.4 18.2 %all_to_all.20.parts_ref = bf16[4,32,3072]{2,1,0:T(8,128)(2,1)S(1)} all-to-all(bf16[4,32,3072]{2,1,0:T(8,128)(2,1)S(1)} %bitcast.19), channel_id=1, replica_groups=mesh['yh'=2,'yl'=2,'xh'=2,'core'=2,'replica'=64] {'xh','yh'}, dimensions={0} | all-to-all | bytes 1572864 | tf_op jit(solution)/shard_map/all_to_all | solution.py:288
  120.8 14.1 %all_to_all.21 = bf16[4,32,3072]{2,1,0:T(8,128)(2,1)S(1)} all-to-all(bf16[4,32,3072]{2,1,0:T(8,128)(2,1)S(1)} %shard_map.131), channel_id=1, replica_groups=mesh['yh'=2,'yl'=2,'xh'=2,'core'=2,'replica'=64] {'xh','yh'}, dimensions={0} | all-to-all | bytes 1572864 | tf_op jit(solution)/shard_map/all_to_all | solution.py:288
  134.9 5.9 %shard_map.132 = bf16[2048,128]{1,0:T(8,128)(2,1)} custom-call(bf16[128,3072]{1,0:T(8,128)(2,1)S(1)} %bitcast.16, bf16[768,1024]{1,0:T(8,128)(2,1)S(1)} %shard_map.129.w0, bf16[768,1024]{1,0:T(8,128)(2,1)} %copy-done.8, bf16[768,1024]{1,0:T(8,128)(2,1)} %copy-done.7, bf16[768,1024]{1,0:T(8,128)(2,1)} %collective-permute-done.2.w3), custom_call_target="tpu_custom_call" | custom-call | flops 805306368 | bytes 6291456 | tf_op jit(solution)/shard_map/pallas_call | solution.py:344
  140.8 20.8 %all-to-all-start.3 = ((bf16[256,8,128]{2,1,0:T(8,128)(2,1)}), bf16[256,8,128]{2,1,0:T(8,128)(2,1)S(1)}, u32[]{:S(2)}, u32[]{:S(2)}) async-start(bf16[256,8,128]{2,1,0:T(8,128)(2,1)} %bitcast.11), calls=%async_computation.3 | async-start | bytes 1048576 | tf_op jit(solution)/shard_map/all_to_all | solution.py:288
  161.5 4.3 %shard_map.134 = (bf16[2,768,1024]{2,1,0:T(8,128)(2,1)}, bf16[2,768,1024]{2,1,0:T(8,128)(2,1)}) custom-call(bf16[128,2048]{1,0:T(8,128)(2,1)} %copy-done.5, bf16[128,3072]{1,0:T(8,128)(2,1)} %bitcast.17), custom_call_target="tpu_custom_call" | custom-call | flops 805306368 | bytes 6291456 | tf_op jit(solution)/shard_map/pallas_call | solution.py:363
  165.8 3.4 %collective-permute-start.3 = (bf16[2,768,1024]{2,1,0:T(8,128)(2,1)}, bf16[2,768,1024]{2,1,0:T(8,128)(2,1)S(1)}, u32[]{:S(2)}, u32[]{:S(2)}) collective-permute-start(bf16[2,768,1024]{2,1,0:T(8,128)(2,1)} %get-tuple-element.25), channel_id=1, source_target_pairs={{0,64},{64,0},{1,65},{65,1},{2,66},{66,2},{3,67},{67,3},{4,68},{68... | collective-permute-start | bytes 9437192 | tf_op jit(solution)/shard_map/ppermute | solution.py:375
  169.2 5.5 %collective-permute-done.3.came_ref = bf16[2,768,1024]{2,1,0:T(8,128)(2,1)S(1)} collective-permute-done((bf16[2,768,1024]{2,1,0:T(8,128)(2,1)}, bf16[2,768,1024]{2,1,0:T(8,128)(2,1)S(1)}, u32[]{:S(2)}, u32[]{:S(2)}) %collective-permute-start.3) | collective-permute-done | bytes 3145760 | tf_op jit(solution)/shard_map/ppermute | solution.py:375
  174.7 1.7 copy-done.9
  176.4 5.9 %shard_map.135 = (bf16[768,1024]{1,0:T(8,128)(2,1)}, bf16[768,1024]{1,0:T(8,128)(2,1)}) custom-call(bf16[2,768,1024]{2,1,0:T(8,128)(2,1)} %get-tuple-element.24.keep_ref, bf16[2,768,1024]{2,1,0:T(8,128)(2,1)} %copy-done.9), custom_call_target="tpu_custom_call" | custom-call | flops 1572864 | bytes 12582912 | tf_op jit(solution)/shard_map/pallas_call | solution.py:376
  182.3 3.0 %collective-permute-start.4 = (bf16[768,1024]{1,0:T(8,128)(2,1)}, bf16[768,1024]{1,0:T(8,128)(2,1)S(1)}, u32[]{:S(2)}, u32[]{:S(2)}) collective-permute-start(bf16[768,1024]{1,0:T(8,128)(2,1)} %get-tuple-element.27), channel_id=1, source_target_pairs={{0,256},{256,0},{1,257},{257,1},{2,258},{258,2},{3,259},{259,3},{4... | collective-permute-start | bytes 4718600 | tf_op jit(solution)/shard_map/ppermute | solution.py:386
  185.4 37.7 %all-to-all-done.3 = bf16[256,8,128]{2,1,0:T(8,128)(2,1)S(1)} async-done(((bf16[256,8,128]{2,1,0:T(8,128)(2,1)}), bf16[256,8,128]{2,1,0:T(8,128)(2,1)S(1)}, u32[]{:S(2)}, u32[]{:S(2)}) %all-to-all-start.3) | async-done | bytes 524320 | tf_op jit(solution)/shard_map/all_to_all | solution.py:288
  224.5 1.5 shard_map.136
  (21 shorter events, 2.9 us)
Async XLA Ops:
  2.9 96.5 %all-to-all-start = ((bf16[256,8,128]{2,1,0:T(8,128)(2,1)}), bf16[256,8,128]{2,1,0:T(8,128)(2,1)S(1)}, u32[]{:S(2)}, u32[]{:S(2)}) async-start(bf16[256,8,128]{2,1,0:T(8,128)(2,1)} %bitcast.24), calls=%async_computation | async-start | bytes 1048576 | tf_op jit(solution)/shard_map/all_to_all | solution.py:288
  37.9 1.0 copy-start.2
  38.9 1.0 copy-start.3
  40.0 1.0 copy-start.4
  41.2 42.5 %collective-permute-start.1 = (bf16[768,1024]{1,0:T(8,128)(2,1)S(1)}, bf16[768,1024]{1,0:T(8,128)(2,1)S(1)}, u32[]{:S(2)}, u32[]{:S(2)}) collective-permute-start(bf16[768,1024]{1,0:T(8,128)(2,1)S(1)} %shard_map.129.w0), channel_id=1, source_target_pairs={{0,256},{256,0},{1,257},{257,1},{2,258},{258,2},{3,259},{259,3},{4... | collective-permute-start | bytes 4718600 | tf_op jit(solution)/shard_map/ppermute | solution.py:317
  45.4 41.8 %collective-permute-start = (bf16[768,1024]{1,0:T(8,128)(2,1)S(1)}, bf16[768,1024]{1,0:T(8,128)(2,1)S(1)}, u32[]{:S(2)}, u32[]{:S(2)}) collective-permute-start(bf16[768,1024]{1,0:T(8,128)(2,1)S(1)} %shard_map.129.w0), channel_id=1, source_target_pairs={{0,64},{64,0},{1,65},{65,1},{2,66},{66,2},{3,67},{67,3},{4,68},{68... | collective-permute-start | bytes 4718600 | tf_op jit(solution)/shard_map/ppermute | solution.py:318
  83.7 3.4 %copy-start.7 = (bf16[768,1024]{1,0:T(8,128)(2,1)}, bf16[768,1024]{1,0:T(8,128)(2,1)S(1)}, u32[]{:S(2)}) copy-start(bf16[768,1024]{1,0:T(8,128)(2,1)S(1)} %collective-permute-done.1.w2) | copy-start | bytes 4718596
  83.7 6.6 %collective-permute-start.2 = (bf16[768,1024]{1,0:T(8,128)(2,1)S(1)}, bf16[768,1024]{1,0:T(8,128)(2,1)}, u32[]{:S(2)}, u32[]{:S(2)}) collective-permute-start(bf16[768,1024]{1,0:T(8,128)(2,1)S(1)} %collective-permute-done.1.w2), channel_id=1, source_target_pairs={{0,64},{64,0},{1,65},{65,1},{2,66},{66,2},{3,67},{67,3},{4,68},{68... | collective-permute-start | bytes 4718600 | tf_op jit(solution)/shard_map/ppermute | solution.py:319
  87.2 1.2 copy-start.8
  102.4 18.4 %copy-start.5 = (bf16[128,2048]{1,0:T(8,128)(2,1)}, bf16[128,2048]{1,0:T(8,128)(2,1)S(1)}, u32[]{:S(2)}) copy-start(bf16[128,2048]{1,0:T(8,128)(2,1)S(1)} %get-tuple-element.23.x_ref) | copy-start | bytes 1572868
  134.9 5.9 %copy-start = (bf16[4,32,3072]{2,1,0:T(8,128)(2,1)}, bf16[4,32,3072]{2,1,0:T(8,128)(2,1)S(1)}, u32[]{:S(2)}) copy-start(bf16[4,32,3072]{2,1,0:T(8,128)(2,1)S(1)} %all_to_all.21) | copy-start | bytes 2359300
  140.8 82.3 %all-to-all-start.3 = ((bf16[256,8,128]{2,1,0:T(8,128)(2,1)}), bf16[256,8,128]{2,1,0:T(8,128)(2,1)S(1)}, u32[]{:S(2)}, u32[]{:S(2)}) async-start(bf16[256,8,128]{2,1,0:T(8,128)(2,1)} %bitcast.11), calls=%async_computation.3 | async-start | bytes 1048576 | tf_op jit(solution)/shard_map/all_to_all | solution.py:288
  165.8 8.8 %collective-permute-start.3 = (bf16[2,768,1024]{2,1,0:T(8,128)(2,1)}, bf16[2,768,1024]{2,1,0:T(8,128)(2,1)S(1)}, u32[]{:S(2)}, u32[]{:S(2)}) collective-permute-start(bf16[2,768,1024]{2,1,0:T(8,128)(2,1)} %get-tuple-element.25), channel_id=1, source_target_pairs={{0,64},{64,0},{1,65},{65,1},{2,66},{66,2},{3,67},{67,3},{4,68},{68... | collective-permute-start | bytes 9437192 | tf_op jit(solution)/shard_map/ppermute | solution.py:375
  174.7 1.7 copy-start.9
  176.4 46.7 %copy-start.6 = (bf16[2,128,256]{2,1,0:T(8,128)(2,1)S(1)}, bf16[2,128,256]{2,1,0:T(8,128)(2,1)}, u32[]{:S(2)}) copy-start(bf16[2,128,256]{2,1,0:T(8,128)(2,1)} %get-tuple-element.18.table_ref) | copy-start | bytes 393220
  182.3 41.7 %collective-permute-start.4 = (bf16[768,1024]{1,0:T(8,128)(2,1)}, bf16[768,1024]{1,0:T(8,128)(2,1)S(1)}, u32[]{:S(2)}, u32[]{:S(2)}) collective-permute-start(bf16[768,1024]{1,0:T(8,128)(2,1)} %get-tuple-element.27), channel_id=1, source_target_pairs={{0,256},{256,0},{1,257},{257,1},{2,258},{258,2},{3,259},{259,3},{4... | collective-permute-start | bytes 4718600 | tf_op jit(solution)/shard_map/ppermute | solution.py:386
  223.1 1.4 copy-start.1

commit v6 on v5

--- a/solution.py
+++ b/solution.py
@@ -39,7 +39,7 @@
 
 
 def me():
-    return lax.axis_index("yl") * 2 + lax.axis_index("core")
+    return lax.axis_index("xh") * 2 + lax.axis_index("core")
 
 
 def pieces(x):
@@ -168,29 +168,19 @@
         out_ref[g, :, 2 * hidden : 3 * hidden] = up_cot
 
 
-def back_kernel(hgu_ref, w0, w1, w2, w3, send_ref, stage_ref, rows_ref, held, sem):
+def back_kernel(hgu_ref, w0, w1, w2, w3, send_ref, stage_ref, rows_ref):
     hidden = w0.shape[1]
     width = w0.shape[0] // 3
-    fetches = []
-    for k, w in enumerate((w0, w1, w2, w3)):
-        for part in range(3):
-            at = pl.ds(part * width, width)
-            fetches.append(
-                pltpu.make_async_copy(w.at[at, :], held.at[k, at, :], sem.at[3 * k + part])
-            )
-            fetches[-1].start()
     blocks = hgu_ref.shape[0] // SLOTS
     peers = QUAD * blocks
     mine = me()
     inner = hgu_ref[:, 0:hidden]
     gate_cot = hgu_ref[:, hidden : 2 * hidden]
     up_cot = hgu_ref[:, 2 * hidden : 3 * hidden]
-    for k in range(QUAD):
-        for fetch in fetches[3 * k : 3 * k + 3]:
-            fetch.wait()
-        out = mm(inner, held[k, 2 * width : 3 * width, :], NT)
-        back = mm(gate_cot, held[k, 0:width, :], NT) + mm(
-            up_cot, held[k, width : 2 * width, :], NT
+    for k, w in enumerate((w0, w1, w2, w3)):
+        out = mm(inner, w[2 * width : 3 * width, :], NT)
+        back = mm(gate_cot, w[0:width, :], NT) + mm(
+            up_cot, w[width : 2 * width, :], NT
         )
         at = pl.ds(pl.multiple_of((mine ^ k) * blocks, blocks), blocks)
         for s in range(SLOTS):
@@ -273,13 +263,13 @@
     count, width = tokens.shape
     hidden = gate_weight.shape[2]
     sources = lax.axis_size("replica")
-    others = ("xh", "yh")
-    groups = lax.axis_size("xh") * lax.axis_size("yh")
+    others = ("yh", "yl")
+    groups = lax.axis_size("yh") * lax.axis_size("yl")
     peers = QUAD * sources
     rows = SLOTS * sources
     shape = jax.ShapeDtypeStruct
     message = shape((peers * TILE, LANE), bf16)
-    everyone = ("yl", "core", "replica")
+    everyone = ("xh", "core", "replica")
     flip = [(0, 1), (1, 0)]
     product = 2 * rows * QUAD * width * hidden
     weight_bytes = 2 * 3 * QUAD * width * hidden
@@ -314,7 +304,7 @@
     w0 = call(gather_kernel, shape((3 * width, hidden), bf16), 0, 12 * width * hidden, ROOM)(
         gate_weight[0], up_weight[0], down_weight[0]
     )
-    w2 = lax.ppermute(w0, "yl", flip)
+    w2 = lax.ppermute(w0, "xh", flip)
     w1 = lax.ppermute(w0, "core", flip)
     w3 = lax.ppermute(w2, "core", flip)
 
@@ -346,14 +336,9 @@
         message,
         3 * product,
         weight_bytes,
-        ROOM,
-        in_specs=[pl.BlockSpec(memory_space=pltpu.VMEM)]
-        + [pl.BlockSpec(memory_space=pl.ANY)] * QUAD,
         scratch_shapes=[
             pltpu.VMEM((TILE, peers, LANE), f32),
             pltpu.VMEM((peers * TILE, LANE), f32),
-            pltpu.VMEM((QUAD, 3 * width, hidden), bf16),
-            pltpu.SemaphoreType.DMA((3 * QUAD,)),
         ],
     )(hgu, w0, w1, w2, w3)
 
@@ -383,7 +368,7 @@
         in_specs=[pl.BlockSpec((2, width // 2, hidden), lambda i: (0, i, 0))] * 2,
         out_specs=[pl.BlockSpec((width // 2, hidden), lambda i: (i, 0))] * 2,
     )(keep, got)
-    theirs = lax.ppermute(other, "yl", flip)
+    theirs = lax.ppermute(other, "xh", flip)
     grads = call(
         last_sum_kernel,
         (

time: 227 us -> 226 us (level)
  starting transfers between devices: 71.8 us -> 79.8 us
  blocking collectives: 32.3 us -> 27 us
  waiting for transfers between devices: 90.4 us -> 87.2 us
    all_to_all x2, blocking collectives: 32.3 us -> 27 us  [spread(): return lax.all_to_all(x, axis, split_axis=0, concat_axis=0, tiled=True)]
    all_to_all x2, starting transfers between devices: 55.7 us -> 60.7 us  [spread(): return lax.all_to_all(x, axis, split_axis=0, concat_axis=0, tiled=True)]
    all_to_all x2, waiting for transfers between devices: 46.8 us -> 42.8 us  [spread(): return lax.all_to_all(x, axis, split_axis=0, concat_axis=0, tiled=True)]
    ppermute x2, starting transfers between devices: 7.18 us -> 10.2 us  [the longest x1 5.64 us: local(): w2 = lax.ppermute(w0, 'xh', flip)]
    unnamed x20 -> x24, local copies, waits for them, and re-layouts: 6.44 us -> 5.99 us
  transfers between devices with their start and end apart: 7 -> 7, of which waited for: 5 -> 6; matrix products, arithmetic and copies ran while one was open for 0% -> 0% of each run, Pallas kernels for 5% -> 5%
where the time goes in v6:
time: 226 us; the launch traced here: 225 us
  waiting for transfers between devices  87.2 us (39%)
  starting transfers between devices  79.8 us (35%)
  blocking collectives  27 us (12%)
  Pallas kernels  24.4 us (11%)
  local copies, waits for them, and re-layouts  5.99 us (3%)
    all_to_all x2, starting transfers between devices, spread(): return lax.all_to_all(x, axis, split_axis=0, concat_axis=0, tiled=True)  60.7 us
    all_to_all x2, waiting for transfers between devices, spread(): return lax.all_to_all(x, axis, split_axis=0, concat_axis=0, tiled=True)  42.8 us
    ppermute x1, waiting for transfers between devices, local(): w2 = lax.ppermute(w0, 'xh', flip)  36.3 us
    all_to_all x2, blocking collectives, spread(): return lax.all_to_all(x, axis, split_axis=0, concat_axis=0, tiled=True)  27 us
    unnamed x24, local copies, waits for them, and re-layouts  5.99 us
    pallas_call x1, Pallas kernels, local(): call(first_sum_kernel, (one, one), 6 * width * hidden, 2 * weight_bytes,...  5.95 us
    ppermute x1, starting transfers between devices, local(): w2 = lax.ppermute(w0, 'xh', flip)  5.64 us
    ppermute x1, waiting for transfers between devices, local(): got = lax.ppermute(give, 'core', flip)  5.47 us
  transfers between devices with their start and end apart: 7, of which 6 were waited for; matrix products, arithmetic and copies ran while one was open for 0% of the time, Pallas kernels for 5%

profile of v6, /device:TPU:1, one launch (start us, length us, event | category | flops | bytes accessed | tf_op | source)
XLA Modules:
  0.0 225.1 jit_solution(17112993238882624615)
XLA Ops:
  0.6 2.3 %shard_map.128 = (bf16[2048,128]{1,0:T(8,128)(2,1)}, bf16[2,128,256]{2,1,0:T(8,128)(2,1)}) custom-call(bf16[32,256]{1,0:T(8,128)(2,1)} %refs_0_.1, bf16[32,256]{1,0:T(8,128)(2,1)} %refs_1_.1, f32[8,32]{1,0:T(8,128)} %bitcast.27, s32[8,32]{1,0:T(8,128)} %bitcast.28, s32[1,32]{1,0:T(1,128)} %bitcast.30, f32[1,256]{1,0:T(1,128)} %bitcast.29), custom_call_target="tpu_custom_call" | custom-call | flops 33554432 | bytes 1048576 | tf_op jit(solution)/shard_map/pallas_call | solution.py:291
  2.9 36.5 %all-to-all-start = ((bf16[256,8,128]{2,1,0:T(8,128)(2,1)}), bf16[256,8,128]{2,1,0:T(8,128)(2,1)}, u32[]{:S(2)}, u32[]{:S(2)}) async-start(bf16[256,8,128]{2,1,0:T(8,128)(2,1)} %bitcast.23), calls=%async_computation | async-start | bytes 1048576 | tf_op jit(solution)/shard_map/all_to_all | solution.py:278
  40.4 1.0 copy-done.7
  41.5 1.0 copy-done.8
  42.7 5.6 %collective-permute-start.1 = (bf16[768,1024]{1,0:T(8,128)(2,1)S(1)}, bf16[768,1024]{1,0:T(8,128)(2,1)S(1)}, u32[]{:S(2)}, u32[]{:S(2)}) collective-permute-start(bf16[768,1024]{1,0:T(8,128)(2,1)S(1)} %shard_map.129.w0), channel_id=1, source_target_pairs={{0,128},{128,0},{1,129},{129,1},{2,130},{130,2},{3,131},{131,3},{4... | collective-permute-start | bytes 4718600 | tf_op jit(solution)/shard_map/ppermute | solution.py:307
  48.4 2.1 collective-permute-start
  50.5 36.3 %collective-permute-done.1.w2 = bf16[768,1024]{1,0:T(8,128)(2,1)S(1)} collective-permute-done((bf16[768,1024]{1,0:T(8,128)(2,1)S(1)}, bf16[768,1024]{1,0:T(8,128)(2,1)S(1)}, u32[]{:S(2)}, u32[]{:S(2)}) %collective-permute-start.1) | collective-permute-done | bytes 1572896 | tf_op jit(solution)/shard_map/ppermute | solution.py:307
  86.8 3.5 %collective-permute-start.2 = (bf16[768,1024]{1,0:T(8,128)(2,1)S(1)}, bf16[768,1024]{1,0:T(8,128)(2,1)}, u32[]{:S(2)}, u32[]{:S(2)}) collective-permute-start(bf16[768,1024]{1,0:T(8,128)(2,1)S(1)} %collective-permute-done.1.w2), channel_id=1, source_target_pairs={{0,64},{64,0},{1,65},{65,1},{2,66},{66,2},{3,67},{67,3},{4,68},{68... | collective-permute-start | bytes 4718600 | tf_op jit(solution)/shard_map/ppermute | solution.py:309
  90.3 1.2 copy-done.2
  91.5 2.0 collective-permute-done.2.w3
  93.5 6.6 %all-to-all-done = bf16[256,8,128]{2,1,0:T(8,128)(2,1)} async-done(((bf16[256,8,128]{2,1,0:T(8,128)(2,1)}), bf16[256,8,128]{2,1,0:T(8,128)(2,1)}, u32[]{:S(2)}, u32[]{:S(2)}) %all-to-all-start) | async-done | bytes 524320 | tf_op jit(solution)/shard_map/all_to_all | solution.py:278
  100.0 4.0 %shard_map.130 = (bf16[128,2048]{1,0:T(8,128)(2,1)S(1)}, bf16[128,3072]{1,0:T(8,128)(2,1)S(1)}) custom-call(bf16[2048,128]{1,0:T(8,128)(2,1)} %bitcast.5.came_ref, bf16[768,1024]{1,0:T(8,128)(2,1)S(1)} %shard_map.129.w0, bf16[768,1024]{1,0:T(8,128)(2,1)} %copy-done.2, bf16[768,1024]{1,0:T(8,128)(2,1)} %copy-done, bf16[768,1024]{1,0:T(8,128)(2,1)} %collective-permute-done.2.w3), custom_call_target="tpu_custom_call" | custom-call | flops 805306368 | bytes 6291456 | tf_op jit(solution)/shard_map/pallas_call | solution.py:311
  104.0 14.7 %all_to_all.20.parts_ref = bf16[4,32,3072]{2,1,0:T(8,128)(2,1)S(1)} all-to-all(bf16[4,32,3072]{2,1,0:T(8,128)(2,1)S(1)} %bitcast.18), channel_id=1, replica_groups=mesh['yh'=2,'yl'=2,'xh'=2,'core'=2,'replica'=64] {'yh','yl'}, dimensions={0} | all-to-all | bytes 1572864 | tf_op jit(solution)/shard_map/all_to_all | solution.py:278
  118.9 12.3 %all_to_all.21 = bf16[4,32,3072]{2,1,0:T(8,128)(2,1)S(1)} all-to-all(bf16[4,32,3072]{2,1,0:T(8,128)(2,1)S(1)} %shard_map.131), channel_id=1, replica_groups=mesh['yh'=2,'yl'=2,'xh'=2,'core'=2,'replica'=64] {'yh','yl'}, dimensions={0} | all-to-all | bytes 1572864 | tf_op jit(solution)/shard_map/all_to_all | solution.py:278
  131.2 5.0 %shard_map.132 = bf16[2048,128]{1,0:T(8,128)(2,1)} custom-call(bf16[128,3072]{1,0:T(8,128)(2,1)S(1)} %bitcast.16, bf16[768,1024]{1,0:T(8,128)(2,1)S(1)} %shard_map.129.w0, bf16[768,1024]{1,0:T(8,128)(2,1)S(1)} %copy-done.3, bf16[768,1024]{1,0:T(8,128)(2,1)S(1)} %copy-done.1, bf16[768,1024]{1,0:T(8,128)(2,1)} %collective-permute-done.2.w3), custom_call_target="tpu_custom_call" | custom-call | flops 805306368 | bytes 6291456 | tf_op jit(solution)/shard_map/pallas_call | solution.py:334
  136.2 24.2 %all-to-all-start.3 = ((bf16[256,8,128]{2,1,0:T(8,128)(2,1)}), bf16[256,8,128]{2,1,0:T(8,128)(2,1)S(1)}, u32[]{:S(2)}, u32[]{:S(2)}) async-start(bf16[256,8,128]{2,1,0:T(8,128)(2,1)} %bitcast.11), calls=%async_computation.3 | async-start | bytes 1048576 | tf_op jit(solution)/shard_map/all_to_all | solution.py:278
  160.4 4.3 %shard_map.134 = (bf16[2,768,1024]{2,1,0:T(8,128)(2,1)}, bf16[2,768,1024]{2,1,0:T(8,128)(2,1)}) custom-call(bf16[128,2048]{1,0:T(8,128)(2,1)} %copy-done.9, bf16[128,3072]{1,0:T(8,128)(2,1)} %bitcast.17), custom_call_target="tpu_custom_call" | custom-call | flops 805306368 | bytes 6291456 | tf_op jit(solution)/shard_map/pallas_call | solution.py:348
  164.7 3.4 %collective-permute-start.3 = (bf16[2,768,1024]{2,1,0:T(8,128)(2,1)}, bf16[2,768,1024]{2,1,0:T(8,128)(2,1)S(1)}, u32[]{:S(2)}, u32[]{:S(2)}) collective-permute-start(bf16[2,768,1024]{2,1,0:T(8,128)(2,1)} %get-tuple-element.25), channel_id=1, source_target_pairs={{0,64},{64,0},{1,65},{65,1},{2,66},{66,2},{3,67},{67,3},{4,68},{68... | collective-permute-start | bytes 9437192 | tf_op jit(solution)/shard_map/ppermute | solution.py:360
  168.1 5.5 %collective-permute-done.3.came_ref = bf16[2,768,1024]{2,1,0:T(8,128)(2,1)S(1)} collective-permute-done((bf16[2,768,1024]{2,1,0:T(8,128)(2,1)}, bf16[2,768,1024]{2,1,0:T(8,128)(2,1)S(1)}, u32[]{:S(2)}, u32[]{:S(2)}) %collective-permute-start.3) | collective-permute-done | bytes 3145760 | tf_op jit(solution)/shard_map/ppermute | solution.py:360
  173.6 1.7 copy-done.11
  175.2 5.9 %shard_map.135 = (bf16[768,1024]{1,0:T(8,128)(2,1)}, bf16[768,1024]{1,0:T(8,128)(2,1)}) custom-call(bf16[2,768,1024]{2,1,0:T(8,128)(2,1)} %get-tuple-element.24.keep_ref, bf16[2,768,1024]{2,1,0:T(8,128)(2,1)} %copy-done.11), custom_call_target="tpu_custom_call" | custom-call | flops 1572864 | bytes 12582912 | tf_op jit(solution)/shard_map/pallas_call | solution.py:361
  181.2 4.5 %collective-permute-start.4 = (bf16[768,1024]{1,0:T(8,128)(2,1)}, bf16[768,1024]{1,0:T(8,128)(2,1)S(1)}, u32[]{:S(2)}, u32[]{:S(2)}) collective-permute-start(bf16[768,1024]{1,0:T(8,128)(2,1)} %get-tuple-element.27), channel_id=1, source_target_pairs={{0,128},{128,0},{1,129},{129,1},{2,130},{130,2},{3,131},{131,3},{4... | collective-permute-start | bytes 4718600 | tf_op jit(solution)/shard_map/ppermute | solution.py:371
  185.7 36.2 %all-to-all-done.3 = bf16[256,8,128]{2,1,0:T(8,128)(2,1)S(1)} async-done(((bf16[256,8,128]{2,1,0:T(8,128)(2,1)}), bf16[256,8,128]{2,1,0:T(8,128)(2,1)S(1)}, u32[]{:S(2)}, u32[]{:S(2)}) %all-to-all-start.3) | async-done | bytes 524320 | tf_op jit(solution)/shard_map/all_to_all | solution.py:278
  223.6 1.5 shard_map.136
  (25 shorter events, 3.1 us)
Async XLA Ops:
  2.9 97.1 %all-to-all-start = ((bf16[256,8,128]{2,1,0:T(8,128)(2,1)}), bf16[256,8,128]{2,1,0:T(8,128)(2,1)}, u32[]{:S(2)}, u32[]{:S(2)}) async-start(bf16[256,8,128]{2,1,0:T(8,128)(2,1)} %bitcast.23), calls=%async_computation | async-start | bytes 1048576 | tf_op jit(solution)/shard_map/all_to_all | solution.py:278
  39.4 1.0 copy-start.6
  40.4 1.0 copy-start.7
  41.5 1.0 copy-start.8
  42.7 44.1 %collective-permute-start.1 = (bf16[768,1024]{1,0:T(8,128)(2,1)S(1)}, bf16[768,1024]{1,0:T(8,128)(2,1)S(1)}, u32[]{:S(2)}, u32[]{:S(2)}) collective-permute-start(bf16[768,1024]{1,0:T(8,128)(2,1)S(1)} %shard_map.129.w0), channel_id=1, source_target_pairs={{0,128},{128,0},{1,129},{129,1},{2,130},{130,2},{3,131},{131,3},{4... | collective-permute-start | bytes 4718600 | tf_op jit(solution)/shard_map/ppermute | solution.py:307
  48.4 41.9 %collective-permute-start = (bf16[768,1024]{1,0:T(8,128)(2,1)S(1)}, bf16[768,1024]{1,0:T(8,128)(2,1)S(1)}, u32[]{:S(2)}, u32[]{:S(2)}) collective-permute-start(bf16[768,1024]{1,0:T(8,128)(2,1)S(1)} %shard_map.129.w0), channel_id=1, source_target_pairs={{0,64},{64,0},{1,65},{65,1},{2,66},{66,2},{3,67},{67,3},{4,68},{68... | collective-permute-start | bytes 4718600 | tf_op jit(solution)/shard_map/ppermute | solution.py:308
  86.8 13.2 %copy-start = (bf16[768,1024]{1,0:T(8,128)(2,1)}, bf16[768,1024]{1,0:T(8,128)(2,1)S(1)}, u32[]{:S(2)}) copy-start(bf16[768,1024]{1,0:T(8,128)(2,1)S(1)} %collective-permute-done.1.w2) | copy-start | bytes 4718596
  86.8 6.6 %collective-permute-start.2 = (bf16[768,1024]{1,0:T(8,128)(2,1)S(1)}, bf16[768,1024]{1,0:T(8,128)(2,1)}, u32[]{:S(2)}, u32[]{:S(2)}) collective-permute-start(bf16[768,1024]{1,0:T(8,128)(2,1)S(1)} %collective-permute-done.1.w2), channel_id=1, source_target_pairs={{0,64},{64,0},{1,65},{65,1},{2,66},{66,2},{3,67},{67,3},{4,68},{68... | collective-permute-start | bytes 4718600 | tf_op jit(solution)/shard_map/ppermute | solution.py:309
  90.3 1.2 copy-start.2
  104.0 14.9 %copy-start.9 = (bf16[128,2048]{1,0:T(8,128)(2,1)}, bf16[128,2048]{1,0:T(8,128)(2,1)S(1)}, u32[]{:S(2)}) copy-start(bf16[128,2048]{1,0:T(8,128)(2,1)S(1)} %get-tuple-element.23.x_ref) | copy-start | bytes 1572868
  118.7 12.5 %copy-start.1 = (bf16[768,1024]{1,0:T(8,128)(2,1)S(1)}, bf16[768,1024]{1,0:T(8,128)(2,1)}, u32[]{:S(2)}) copy-start(bf16[768,1024]{1,0:T(8,128)(2,1)} %copy-done) | copy-start | bytes 4718596
  118.7 12.5 %copy-start.3 = (bf16[768,1024]{1,0:T(8,128)(2,1)S(1)}, bf16[768,1024]{1,0:T(8,128)(2,1)}, u32[]{:S(2)}) copy-start(bf16[768,1024]{1,0:T(8,128)(2,1)} %copy-done.2) | copy-start | bytes 4718596
  131.2 5.0 %copy-start.4 = (bf16[4,32,3072]{2,1,0:T(8,128)(2,1)}, bf16[4,32,3072]{2,1,0:T(8,128)(2,1)S(1)}, u32[]{:S(2)}) copy-start(bf16[4,32,3072]{2,1,0:T(8,128)(2,1)S(1)} %all_to_all.21) | copy-start | bytes 2359300
  136.2 85.7 %all-to-all-start.3 = ((bf16[256,8,128]{2,1,0:T(8,128)(2,1)}), bf16[256,8,128]{2,1,0:T(8,128)(2,1)S(1)}, u32[]{:S(2)}, u32[]{:S(2)}) async-start(bf16[256,8,128]{2,1,0:T(8,128)(2,1)} %bitcast.11), calls=%async_computation.3 | async-start | bytes 1048576 | tf_op jit(solution)/shard_map/all_to_all | solution.py:278
  164.7 8.8 %collective-permute-start.3 = (bf16[2,768,1024]{2,1,0:T(8,128)(2,1)}, bf16[2,768,1024]{2,1,0:T(8,128)(2,1)S(1)}, u32[]{:S(2)}, u32[]{:S(2)}) collective-permute-start(bf16[2,768,1024]{2,1,0:T(8,128)(2,1)} %get-tuple-element.25), channel_id=1, source_target_pairs={{0,64},{64,0},{1,65},{65,1},{2,66},{66,2},{3,67},{67,3},{4,68},{68... | collective-permute-start | bytes 9437192 | tf_op jit(solution)/shard_map/ppermute | solution.py:360
  173.6 1.7 copy-start.11
  175.2 46.7 %copy-start.10 = (bf16[2,128,256]{2,1,0:T(8,128)(2,1)S(1)}, bf16[2,128,256]{2,1,0:T(8,128)(2,1)}, u32[]{:S(2)}) copy-start(bf16[2,128,256]{2,1,0:T(8,128)(2,1)} %get-tuple-element.18.table_ref) | copy-start | bytes 393220
  181.2 42.4 %collective-permute-start.4 = (bf16[768,1024]{1,0:T(8,128)(2,1)}, bf16[768,1024]{1,0:T(8,128)(2,1)S(1)}, u32[]{:S(2)}, u32[]{:S(2)}) collective-permute-start(bf16[768,1024]{1,0:T(8,128)(2,1)} %get-tuple-element.27), channel_id=1, source_target_pairs={{0,128},{128,0},{1,129},{129,1},{2,130},{130,2},{3,131},{131,3},{4... | collective-permute-start | bytes 4718600 | tf_op jit(solution)/shard_map/ppermute | solution.py:371
  221.9 1.6 copy-start.5
